TPU v7x, 128 devices: a whole 4x4x4 slice. The times are simulated.
128 devices in a mesh: ctx: 32 (over x, y_lo, z), tp: 4 (over y_hi, core).
Axes of the slice: x: 4, y: 4 (y_hi: 2, y_lo: 2; y = y_hi * 2 + y_lo), z: 4, core: 2. Of those that a mesh axis runs over, the one named last changes fastest.
Arguments:
- projected: bfloat16 [3, 4096, 4096], P(None, 'tp', 'ctx'), may hold values from -6 to 6
- conv_weight: float32 [7, 3, 4096], P(None, None, 'tp'), may hold values from -2 to 2
- filters: float32 [4, 64, 4096], P('tp', 'ctx'), may hold values from -6 to 6
- skip_gain: float32 [4096], P('tp'), may hold values from -1 to 1
- out_weight: bfloat16 [4096, 4096], P('tp', 'ctx'), may hold values from -0.09375 to 0.09375
- cotangent: bfloat16 [4096, 4096], P('tp', 'ctx'), may hold values from -6 to 6
Outputs:
- block_out: bfloat16 [4096, 4096], P('tp', 'ctx')
- proj_grad: bfloat16 [3, 4096, 4096], P(None, 'tp', 'ctx')
- filter_grad: float32 [4, 64, 4096], P('tp', 'ctx')
All inputs are finite; a program needn't handle non-finite values.
Results may differ from a plain program's by a relative error of at most 0.017.
Values may be sent and summed in bfloat16 or wider, within the bound.
A program may use at most 128 MiB of HBM per device.

v0:
```python
import math

import jax
import jax.numpy as jnp
from jax import lax
from jax.sharding import PartitionSpec as P

GROUP = 16


precise = lax.Precision.HIGHEST


def from_behind(block, axis, distance):
    devices = range(lax.axis_size(axis))
    route = [(i - distance, i) for i in devices if i - distance in devices]
    return lax.ppermute(block, axis, route)


def rims(edge_rows, step_by):
    return from_behind(edge_rows, "ctx", step_by)


def short_forward(projected, prev_rim, conv_weight):
    kernel = conv_weight.shape[0]
    tokens = projected.shape[2]
    extended = jnp.concatenate([prev_rim, projected], axis=2)
    summed = jnp.zeros(projected.shape, jnp.float32)
    for offset in range(kernel):
        begin_at = kernel - 1 - offset
        summed = summed + conv_weight[offset][:, :, None] * extended[
            :, :, begin_at : begin_at + tokens
        ].astype(jnp.float32)
    return summed.astype(jnp.bfloat16)


def short_backward(dshort, next_rim, conv_weight):
    kernel = conv_weight.shape[0]
    tokens = dshort.shape[2]
    extended = jnp.concatenate([dshort, next_rim], axis=2)
    summed = jnp.zeros(dshort.shape, jnp.float32)
    for offset in range(kernel):
        summed = summed + conv_weight[offset][:, :, None] * extended[
            :, :, offset : offset + tokens
        ].astype(jnp.float32)
    return summed.astype(jnp.bfloat16)


def to_owners(values_in, ctx_size):
    channels, tokens = values_in.shape
    arrived = lax.all_to_all(
        values_in.reshape(ctx_size, channels // ctx_size, 1, tokens),
        "ctx",
        split_axis=0,
        concat_axis=2,
        tiled=True,
    )
    return arrived.reshape(channels // ctx_size, ctx_size, tokens)


def to_tokens(values_in):
    own_width, ctx_size, tokens = values_in.shape
    arrived = lax.all_to_all(
        values_in.reshape(1, own_width, ctx_size, tokens),
        "ctx",
        split_axis=2,
        concat_axis=0,
        tiled=True,
    )
    return arrived.reshape(ctx_size * own_width, tokens)


def split_factor(length):
    first = 1
    while first * first * 4 <= length and length % (first * 2) == 0:
        first = first * 2
    return first


def rotation(rows, cols, modulus, sign):
    row_ids = lax.iota(jnp.int32, rows)
    col_ids = lax.iota(jnp.int32, cols)
    angle = (
        2.0
        * math.pi
        * (row_ids[:, None] * col_ids[None, :] % modulus).astype(jnp.float32)
        / modulus
    )
    return (jnp.cos(angle), sign * jnp.sin(angle))


def long_dft(part_re, part_im, sign):
    length = part_re.shape[-1]
    first = split_factor(length)
    second = length // first
    lead = part_re.shape[:-1]
    part_re = part_re.reshape(lead + (first, second))
    part_im = part_im.reshape(lead + (first, second))
    cos_a, sin_a = rotation(first, first, first, sign)
    y_re = jnp.einsum("...pm,pl->...lm", part_re, cos_a, precision=precise) - jnp.einsum(
        "...pm,pl->...lm", part_im, sin_a, precision=precise
    )
    y_im = jnp.einsum("...pm,pl->...lm", part_re, sin_a, precision=precise) + jnp.einsum(
        "...pm,pl->...lm", part_im, cos_a, precision=precise
    )
    tw_c, tw_s = rotation(first, second, length, sign)
    z_re = y_re * tw_c - y_im * tw_s
    z_im = y_re * tw_s + y_im * tw_c
    cos_b, sin_b = rotation(second, second, second, sign)
    w_re = jnp.einsum("...lm,mk->...kl", z_re, cos_b, precision=precise) - jnp.einsum(
        "...lm,mk->...kl", z_im, sin_b, precision=precise
    )
    w_im = jnp.einsum("...lm,mk->...kl", z_re, sin_b, precision=precise) + jnp.einsum(
        "...lm,mk->...kl", z_im, cos_b, precision=precise
    )
    return (w_re.reshape(lead + (length,)), w_im.reshape(lead + (length,)))


def spectral_tables(ctx_size, tokens):
    doubled = 2 * ctx_size
    full_len = doubled * tokens
    freq_rows = lax.iota(jnp.int32, doubled)
    src_rows = lax.iota(jnp.int32, ctx_size)
    tok_cols = lax.iota(jnp.int32, tokens)
    two_pi = 2.0 * math.pi
    angle_p = (
        two_pi * (freq_rows[:, None] * src_rows[None, :] % doubled).astype(jnp.float32) / doubled
    )
    angle_t = (
        two_pi * (freq_rows[:, None] * tok_cols[None, :] % full_len).astype(jnp.float32) / full_len
    )
    return (jnp.cos(angle_p), jnp.sin(angle_p), jnp.cos(angle_t), jnp.sin(angle_t), full_len)


def forward_spec(values_in, tables):
    cos_p, sin_p, tw_cos, tw_sin, full_len = tables
    b_re = jnp.einsum("kn,bnm->bkm", cos_p, values_in, precision=precise)
    b_im = -jnp.einsum("kn,bnm->bkm", sin_p, values_in, precision=precise)
    c_re = b_re * tw_cos + b_im * tw_sin
    c_im = b_im * tw_cos - b_re * tw_sin
    return long_dft(c_re, c_im, -1.0)


def inverse_spec(x_re, x_im, tables):
    cos_p, sin_p, tw_cos, tw_sin, full_len = tables
    c_re, c_im = long_dft(x_re, x_im, 1.0)
    b_re = c_re * tw_cos - c_im * tw_sin
    b_im = c_re * tw_sin + c_im * tw_cos
    result = jnp.einsum("kn,bkm->bnm", cos_p, b_re, precision=precise) - jnp.einsum(
        "kn,bkm->bnm", sin_p, b_im, precision=precise
    )
    return result * (1.0 / full_len)


def forward_part(mix_own, own_taps, skip_own, tables):
    own_width, ctx_size, tokens = mix_own.shape
    mix_vals = mix_own.astype(jnp.float32)
    m_re, m_im = forward_spec(mix_vals, tables)
    h_re, h_im = forward_spec(own_taps.reshape(-1, ctx_size, tokens), tables)
    groups = h_re.shape[0]
    m_re = m_re.reshape(groups, GROUP, 2 * ctx_size, tokens)
    m_im = m_im.reshape(groups, GROUP, 2 * ctx_size, tokens)
    h_re = h_re[:, None]
    h_im = h_im[:, None]
    p_re = (m_re * h_re - m_im * h_im).reshape(own_width, 2 * ctx_size, tokens)
    p_im = (m_re * h_im + m_im * h_re).reshape(own_width, 2 * ctx_size, tokens)
    convolved = inverse_spec(p_re, p_im, tables)
    long_own = (convolved + skip_own[:, None, None] * mix_vals).astype(jnp.bfloat16)
    return (long_own, (m_re, m_im, h_re, h_im))


def backward_part(dlong_own, spectra, skip_own, tables):
    m_re, m_im, h_re, h_im = spectra
    own_width, ctx_size, tokens = dlong_own.shape
    groups = m_re.shape[0]
    dlong_vals = dlong_own.astype(jnp.float32)
    d_re, d_im = forward_spec(dlong_vals, tables)
    d_re = d_re.reshape(groups, GROUP, 2 * ctx_size, tokens)
    d_im = d_im.reshape(groups, GROUP, 2 * ctx_size, tokens)
    q_re = (d_re * h_re + d_im * h_im).reshape(own_width, 2 * ctx_size, tokens)
    q_im = (d_im * h_re - d_re * h_im).reshape(own_width, 2 * ctx_size, tokens)
    correlated = inverse_spec(q_re, q_im, tables)
    dmix_own = (correlated + skip_own[:, None, None] * dlong_vals).astype(jnp.bfloat16)
    g_re = jnp.sum(d_re * m_re + d_im * m_im, axis=1)
    g_im = jnp.sum(d_im * m_re - d_re * m_im, axis=1)
    scaling = 1.0 / math.sqrt(GROUP * ctx_size * tokens)
    filter_grad = inverse_spec(g_re, g_im, tables) * scaling
    return (dmix_own, filter_grad.reshape(1, groups, ctx_size * tokens))


def local(projected, conv_weight, filters, skip_gain, out_weight, cotangent):
    kernel = conv_weight.shape[0]
    channels = projected.shape[1]
    tokens = projected.shape[2]
    ctx_size = lax.axis_size("ctx")
    own_width = channels // ctx_size
    weight_full = lax.all_gather(out_weight, "ctx", axis=1, tiled=True)
    prev_rim = rims(projected[:, :, tokens - (kernel - 1) :], 1)
    short_out = short_forward(projected, prev_rim, conv_weight)
    mix_input = (short_out[1].astype(jnp.float32) * short_out[2].astype(jnp.float32)).astype(
        jnp.bfloat16
    )
    weight_cols = weight_full
    dgated = jnp.dot(
        weight_cols,
        lax.all_gather(cotangent, "tp", axis=0, tiled=True),
        preferred_element_type=jnp.float32,
    ).astype(jnp.bfloat16)
    dlongmix = (dgated.astype(jnp.float32) * short_out[0].astype(jnp.float32)).astype(jnp.bfloat16)
    tables = spectral_tables(ctx_size, tokens)
    skip_own = lax.dynamic_slice_in_dim(skip_gain, lax.axis_index("ctx") * own_width, own_width)
    own_taps = filters[0]
    mix_own = to_owners(mix_input, ctx_size)
    long_own, spectra = forward_part(mix_own, own_taps, skip_own, tables)
    longmix = to_tokens(long_own)
    dlong_own = to_owners(dlongmix, ctx_size)
    dmix_own, filter_grad = backward_part(dlong_own, spectra, skip_own, tables)
    dmix_input = to_tokens(dmix_own)
    gated_out = (short_out[0].astype(jnp.float32) * longmix.astype(jnp.float32)).astype(
        jnp.bfloat16
    )
    weight_cols = weight_full
    block_out = lax.psum_scatter(
        lax.dot_general(
            weight_cols, gated_out, (((0,), (0,)), ((), ())), preferred_element_type=jnp.float32
        ).astype(jnp.bfloat16),
        "tp",
        scatter_dimension=0,
        tiled=True,
    )
    dmix_vals = dmix_input.astype(jnp.float32)
    dshort = jnp.stack(
        [
            dgated.astype(jnp.float32) * longmix.astype(jnp.float32),
            dmix_vals * short_out[2].astype(jnp.float32),
            dmix_vals * short_out[1].astype(jnp.float32),
        ]
    ).astype(jnp.bfloat16)
    next_rim = rims(dshort[:, :, : kernel - 1], -1)
    proj_grad = short_backward(dshort, next_rim, conv_weight)
    return (block_out, proj_grad, filter_grad)


def solution(mesh):
    return jax.shard_map(
        local,
        mesh=mesh,
        in_specs=(
            P(None, "tp", "ctx"),
            P(None, None, "tp"),
            P("tp", "ctx", None),
            P("tp"),
            P("tp", "ctx"),
            P("tp", "ctx"),
        ),
        out_specs=(P("tp", "ctx"), P(None, "tp", "ctx"), P("tp", "ctx", None)),
        check_vma=False,
    )
```

profile of v0, /device:TPU:0, one launch (start us, length us, event | category | flops | bytes accessed | tf_op | source)
XLA Modules:
  0.0 461.9 jit_solution(14829311286853320796)
XLA Ops:
  10.1 3.9 collective-permute-start
  19.6 8.7 %all-to-all-start = ((bf16[32,32,1,128]{3,1,2,0:T(8,128)(2,1)}), bf16[32,32,1,128]{3,1,2,0:T(8,128)(2,1)S(1)}, u32[]{:S(2)}, u32[]{:S(2)}) async-start(bf16[32,32,1,128]{3,1,2,0:T(8,128)(2,1)} %bitcast.8), calls=%async_computation | async-start | bytes 524288 | tf_op jit(solution)/shard_map/all_to_all | solution.py:51
  32.3 5.3 %all-to-all-done = bf16[32,32,1,128]{3,1,2,0:T(8,128)(2,1)S(1)} async-done(((bf16[32,32,1,128]{3,1,2,0:T(8,128)(2,1)}), bf16[32,32,1,128]{3,1,2,0:T(8,128)(2,1)S(1)}, u32[]{:S(2)}, u32[]{:S(2)}) %all-to-all-start) | async-done | bytes 262176 | tf_op jit(solution)/shard_map/all_to_all | solution.py:51
  38.3 166.0 %all-gather.3.cloned.1.call-done = bf16[1024,4096]{1,0:T(8,128)(2,1)} async-done(((bf16[1024,128]{1,0:T(8,128)(2,1)}), bf16[1024,4096]{1,0:T(8,128)(2,1)}) %all-gather.3.cloned.1.call-update) | async-done | bytes 8388624 | tf_op jit(solution)/shard_map/all_gather | solution.py:197
  204.3 7.3 %fusion.151 = (bf16[1024,128]{0,1:T(8,128)(2,1)S(1)}, f32[1024,128]{0,1:T(8,128)}) fusion(bf16[3,1024,128]{1,2,0:T(8,128)(2,1)S(1)} %add_convert_fusion.1, bf16[1024,4096]{1,0:T(8,128)(2,1)} %all-gather.3.cloned.1.call-done, bf16[4096,128]{1,0:T(8,128)(2,1)} %all-gather.5.cloned.1.call-done), kind=kOutput, calls=%fused_computation.189 | convolution fusion | flops 1074397184 | bytes 10485760 | tf_op jit(solution)/shard_map/dot_general | solution.py:204
  212.5 9.5 %all-to-all-start.2 = ((bf16[32,32,1,128]{3,1,2,0:T(8,128)(2,1)}), bf16[32,32,1,128]{3,1,2,0:T(8,128)(2,1)S(1)}, u32[]{:S(2)}, u32[]{:S(2)}) async-start(bf16[32,32,1,128]{3,1,2,0:T(8,128)(2,1)} %bitcast.68), calls=%async_computation.3 | async-start | bytes 524288 | tf_op jit(solution)/shard_map/all_to_all | solution.py:51
  223.7 7.1 %all-to-all-done.2 = bf16[32,32,1,128]{3,1,2,0:T(8,128)(2,1)S(1)} async-done(((bf16[32,32,1,128]{3,1,2,0:T(8,128)(2,1)}), bf16[32,32,1,128]{3,1,2,0:T(8,128)(2,1)S(1)}, u32[]{:S(2)}, u32[]{:S(2)}) %all-to-all-start.2) | async-done | bytes 262176 | tf_op jit(solution)/shard_map/all_to_all | solution.py:51
  231.5 3.9 multiply_add_fusion.1
  237.2 3.6 fusion.63
  240.8 3.6 fusion.61
  246.2 3.7 fusion.29
  249.8 3.8 fusion.31
  255.5 5.3 %fusion.69 = f32[8,32,64,16]{2,0,3,1:T(8,128)} fusion(f32[8,32,64,16]{2,0,3,1:T(8,128)} %fusion.63, f32[32,64,8,16]{1,3,2,0:T(8,128)S(1)} %bitcast.395), kind=kOutput, calls=%fused_computation.105 | convolution fusion | flops 25428864 | bytes 3145728 | tf_op jit(solution)/shard_map/...pm,pl->...lm/dot_general | solution.py:100
  260.8 3.7 fusion.72
  265.1 4.1 fusion.92
  269.3 4.9 %subtract_bitcast_fusion.3 = (f32[32,64,8,16]{1,2,3,0:T(8,128)S(1)}, f32[32,64,8,16]{1,2,3,0:T(8,128)S(1)}, f32[32,64,8,16]{1,2,3,0:T(8,128)S(1)}, f32[32,64,8,16]{1,2,3,0:T(8,128)S(1)}) fusion(f32[8,32,64,16]{2,0,3,1:T(8,128)S(1)} %fusion.92, f32[8,16]{0,1:T(8,128)} %get-tuple-element.66, f32[8,16]{0,1:T(8,128)} %get-tuple-element.67, ...), kind=kOutput, calls=%fused_computation.27 | convolution fusion | flops 28574592 | bytes 9438208 | tf_op jit(solution)/shard_map/...pm,pl->...lm/dot_general | solution.py:100
  286.2 2.4 add_bitcast_fusion.2
  288.6 4.6 %multiply_subtract_fusion = (f32[32,64,16,8]{1,2,3,0:T(8,128)}, f32[32,64,16,8]{1,2,3,0:T(8,128)S(1)}, f32[32,64,16,8]{1,2,3,0:T(8,128)}) fusion(f32[32,64,16,8]{1,2,3,0:T(8,128)S(1)} %add_bitcast_fusion.6, f32[32,64,16,8]{1,2,3,0:T(8,128)S(1)} %add_bitcast_fusion.2, f32[32,64,16,8]{1,2,3,0:T(8,128)S(1)} %subtract_bitcast_fusion.6, ...), kind=kOutput, calls=%fused_computation.18 | convolution fusion | flops 52170240 | bytes 8388608 | tf_op jit(solution)/shard_map/...lm,mk->...kl/dot_general | solution.py:110
  297.9 3.8 copy.232
  310.0 2.3 copy.211
  315.2 2.4 copy.208
  320.7 4.9 %fusion.1 = (f32[32,64,8,16]{1,3,2,0:T(8,128)S(1)}, f32[32,64,8,16]{1,3,2,0:T(8,128)S(1)}, f32[32,64,8,16]{1,3,2,0:T(8,128)S(1)}, f32[32,64,8,16]{1,3,2,0:T(8,128)S(1)}) fusion(f32[32,64,8,16]{1,3,2,0:T(8,128)} %bitcast.408, f32[32,64,8,16]{1,3,2,0:T(8,128)} %bitcast.407, f32[32,64,8,16]{1,3,2,0:T(8,128)S(1)} %bitcast.404, f32[32,64,8,16]{1,3,2,0:T(8,128)} %bitcast.406, ...), kind=kLoop, calls=%fused_computation.4 | loop fusion | flops 3145728 | bytes 10485760 | tf_op jit(solution)/shard_map/add | solution.py:180
  325.7 2.3 fusion.47
  328.0 2.3 fusion.45
  332.5 2.3 fusion.13
  334.8 2.6 fusion.79
  337.4 2.3 fusion.82
  339.8 2.4 fusion.99
  342.2 3.9 subtract_bitcast_fusion.1
  346.1 2.4 fusion.7
  348.5 3.3 fusion.5
  351.8 3.4 fusion.39
  355.2 3.3 fusion.37
  364.9 4.3 add_bitcast_fusion
  369.2 2.4 copy.459
  371.5 3.2 copy.223
  374.7 3.6 subtract_bitcast_fusion.4
  378.3 2.3 copy.462
  380.6 3.2 copy.186
  383.8 3.7 add_bitcast_fusion.4
  393.8 2.3 fusion.121
  397.0 4.1 all-to-all-start.1
  404.8 5.4 %all-to-all-done.1 = bf16[1,32,32,128]{3,1,0,2:T(8,128)(2,1)S(1)} async-done(((bf16[1,32,32,128]{3,1,0,2:T(8,128)(2,1)}), bf16[1,32,32,128]{3,1,0,2:T(8,128)(2,1)S(1)}, u32[]{:S(2)}, u32[]{:S(2)}) %all-to-all-start.1) | async-done | bytes 262176 | tf_op jit(solution)/shard_map/all_to_all | solution.py:63
  410.3 3.9 all-to-all-start.3
  414.5 5.6 %fusion = bf16[4096,128]{0,1:T(8,128)(2,1)} fusion(bf16[1024,4096]{1,0:T(8,128)(2,1)} %all-gather.3.cloned.1.call-done, f32[1024,128]{0,1:T(8,128)S(1)} %copy.195, bf16[3,1024,128]{1,2,0:T(8,128)(2,1)S(1)} %copy-done.9), kind=kOutput, calls=%fused_computation.1 | convolution fusion | flops 1074659328 | bytes 10223616 | tf_op jit(solution)/shard_map/dot_general | solution.py:224
  420.9 2.5 all-to-all-done.3
  426.3 3.7 collective-permute-done.1
  432.7 20.6 %reduce-scatter.2.cloned.1.call-done = bf16[1024,128]{0,1:T(8,128)(2,1)} async-done(((bf16[4096,128]{0,1:T(8,128)(2,1)}), bf16[1024,128]{0,1:T(8,128)(2,1)}) %reduce-scatter.2.cloned.1.call-update) | async-done | bytes 262160 | tf_op jit(solution)/shard_map/reduce_scatter | solution.py:223
  (182 shorter events, 80.9 us)
Async XLA Ops:
  7.2 7.0 %copy-start.40 = (f32[1,2,4096]{2,1,0:T(2,128)S(1)}, f32[1,2,4096]{2,1,0:T(2,128)}, u32[]{:S(2)}) copy-start(f32[1,2,4096]{2,1,0:T(2,128)} %param.8) | copy-start | bytes 98308
  7.2 7.8 %copy-start.41 = (f32[7,3,1024]{2,0,1:T(8,128)S(1)}, f32[7,3,1024]{2,0,1:T(8,128)}, u32[]{:S(2)}) copy-start(f32[7,3,1024]{2,0,1:T(8,128)} %param.7) | copy-start | bytes 258052
  7.2 31.1 %all-gather.5.cloned.1.call-start = ((), (), s32[]{:S(2)}) async-start(), calls=%async_computation.7 | async-start | bytes 1310720 | tf_op jit(solution)/shard_map/all_gather | solution.py:206
  7.9 196.4 %all-gather.3.cloned.1.call-start = ((), (), s32[]{:S(2)}) async-start(), calls=%async_computation.5 | async-start | bytes 8650752 | tf_op jit(solution)/shard_map/all_gather | solution.py:197
  10.1 7.0 %collective-permute-start = (bf16[3,1024,6]{1,2,0:T(8,128)(2,1)S(1)}, bf16[3,1024,6]{1,2,0:T(8,128)(2,1)S(1)}, u32[]{:S(2)}, u32[]{:S(2)}) collective-permute-start(bf16[3,1024,6]{1,2,0:T(8,128)(2,1)S(1)} %slice.106), channel_id=1, source_target_pairs={{0,4},{4,8},{8,12},{12,16},{16,20},{20,24},{24,28},{28,32},{32,36}... | collective-permute-start | bytes 110600 | tf_op jit(solution)/shard_map/ppermute | solution.py:17
  15.1 4.5 copy-start.27
  15.1 4.5 copy-start.29
  15.1 4.5 copy-start.31
  15.1 13.2 %copy-start.33 = (f32[3,1024]{1,0:T(4,128)}, f32[3,1024]{1,0:T(4,128)S(1)}, u32[]{:S(2)}) copy-start(f32[3,1024]{1,0:T(4,128)S(1)} %get-tuple-element.62) | copy-start | bytes 36868
  15.1 14.0 %copy-start.35 = (f32[3,1024]{1,0:T(4,128)}, f32[3,1024]{1,0:T(4,128)S(1)}, u32[]{:S(2)}) copy-start(f32[3,1024]{1,0:T(4,128)S(1)} %get-tuple-element.63) | copy-start | bytes 36868
  17.1 15.2 %copy-start.37 = (f32[1,3,1024]{2,1,0:T(4,128)}, f32[1,3,1024]{2,1,0:T(4,128)S(1)}, u32[]{:S(2)}) copy-start(f32[1,3,1024]{2,1,0:T(4,128)S(1)} %copy.465) | copy-start | bytes 36868
  18.6 193.0 %copy-start.8 = (bf16[3,1024,128]{1,2,0:T(8,128)(2,1)}, bf16[3,1024,128]{1,2,0:T(8,128)(2,1)S(1)}, u32[]{:S(2)}) copy-start(bf16[3,1024,128]{1,2,0:T(8,128)(2,1)S(1)} %add_convert_fusion.1) | copy-start | bytes 2359300
  19.6 18.0 %all-to-all-start = ((bf16[32,32,1,128]{3,1,2,0:T(8,128)(2,1)}), bf16[32,32,1,128]{3,1,2,0:T(8,128)(2,1)S(1)}, u32[]{:S(2)}, u32[]{:S(2)}) async-start(bf16[32,32,1,128]{3,1,2,0:T(8,128)(2,1)} %bitcast.8), calls=%async_computation | async-start | bytes 524288 | tf_op jit(solution)/shard_map/all_to_all | solution.py:51
  212.5 18.3 %all-to-all-start.2 = ((bf16[32,32,1,128]{3,1,2,0:T(8,128)(2,1)}), bf16[32,32,1,128]{3,1,2,0:T(8,128)(2,1)S(1)}, u32[]{:S(2)}, u32[]{:S(2)}) async-start(bf16[32,32,1,128]{3,1,2,0:T(8,128)(2,1)} %bitcast.68), calls=%async_computation.3 | async-start | bytes 524288 | tf_op jit(solution)/shard_map/all_to_all | solution.py:51
  230.8 4.6 copy-start.16
  255.5 5.3 %copy-start.11 = (f32[8,32,64,16]{2,0,3,1:T(8,128)S(1)}, f32[8,32,64,16]{2,0,3,1:T(8,128)}, u32[]{:S(2)}) copy-start(f32[8,32,64,16]{2,0,3,1:T(8,128)} %fusion.61) | copy-start | bytes 3145732
  265.1 4.2 copy-start.12
  265.1 4.2 copy-start.13
  265.1 4.2 copy-start.15
  284.2 4.5 copy-start.1
  288.6 4.6 %copy-start.3 = (f32[32,64,16,8]{1,2,3,0:T(8,128)}, f32[32,64,16,8]{1,2,3,0:T(8,128)S(1)}, u32[]{:S(2)}) copy-start(f32[32,64,16,8]{1,2,3,0:T(8,128)S(1)} %add_bitcast_fusion.2) | copy-start | bytes 3145732
  301.7 2.5 copy-start.21
  301.7 2.5 copy-start.23
  301.7 2.5 copy-start.24
  303.5 4.9 %copy-start.2 = (f32[32,64,16,8]{1,2,3,0:T(8,128)S(1)}, f32[32,64,16,8]{1,2,3,0:T(8,128)}, u32[]{:S(2)}) copy-start(f32[32,64,16,8]{1,2,3,0:T(8,128)} %copy-done.1) | copy-start | bytes 3145732
  312.3 2.9 copy-start.14
  317.6 3.1 copy-start.10
  339.7 2.4 copy-start.39
  346.1 12.4 %copy-start = (f32[32,64,8,16]{1,2,3,0:T(8,128)}, f32[32,64,8,16]{1,2,3,0:T(8,128)S(1)}, u32[]{:S(2)}) copy-start(f32[32,64,8,16]{1,2,3,0:T(8,128)S(1)} %get-tuple-element.18) | copy-start | bytes 3145732
  389.6 3.3 copy-start.6
  393.8 7.2 %copy-start.5 = (f32[32,64,128]{2,1,0:T(8,128)S(1)}, f32[32,64,128]{2,1,0:T(8,128)}, u32[]{:S(2)}) copy-start(f32[32,64,128]{2,1,0:T(8,128)} %copy.223) | copy-start | bytes 3145732
  396.1 5.8 %copy-start.17 = (bf16[32,32,1,128]{3,1,2,0:T(8,128)(2,1)S(1)}, bf16[32,32,1,128]{3,1,2,0:T(8,128)(2,1)}, u32[]{:S(2)}) copy-start(bf16[32,32,1,128]{3,1,2,0:T(8,128)(2,1)} %copy-done.16) | copy-start | bytes 786436
  397.0 13.3 %all-to-all-start.1 = ((bf16[1,32,32,128]{3,1,0,2:T(8,128)(2,1)}), bf16[1,32,32,128]{3,1,0,2:T(8,128)(2,1)S(1)}, u32[]{:S(2)}, u32[]{:S(2)}) async-start(bf16[1,32,32,128]{3,1,0,2:T(8,128)(2,1)} %copy.193), calls=%async_computation.1 | async-start | bytes 524288 | tf_op jit(solution)/shard_map/all_to_all | solution.py:63
  402.0 2.5 copy-start.19
  402.0 2.5 copy-start.26
  403.7 10.8 %copy-start.9 = (bf16[3,1024,128]{1,2,0:T(8,128)(2,1)S(1)}, bf16[3,1024,128]{1,2,0:T(8,128)(2,1)}, u32[]{:S(2)}) copy-start(bf16[3,1024,128]{1,2,0:T(8,128)(2,1)} %copy-done.8) | copy-start | bytes 2359300
  410.3 13.1 %all-to-all-start.3 = ((bf16[1,32,32,128]{3,1,0,2:T(8,128)(2,1)}), bf16[1,32,32,128]{3,1,0,2:T(8,128)(2,1)S(1)}, u32[]{:S(2)}, u32[]{:S(2)}) async-start(bf16[1,32,32,128]{3,1,0,2:T(8,128)(2,1)} %copy.226), calls=%async_computation.4 | async-start | bytes 524288 | tf_op jit(solution)/shard_map/all_to_all | solution.py:63
  414.1 39.2 %reduce-scatter.2.cloned.1.call-start = ((), (), s32[]{:S(2)}) async-start(), calls=%async_computation.6 | async-start | bytes 1310720 | tf_op jit(solution)/shard_map/reduce_scatter | solution.py:223
  414.5 5.7 %copy-start.25 = (f32[16,2,64,8]{2,0,3,1:T(8,128)S(1)}, f32[16,2,64,8]{2,0,3,1:T(8,128)}, u32[]{:S(2)}) copy-start(f32[16,2,64,8]{2,0,3,1:T(8,128)} %fusion.183) | copy-start | bytes 196612
  414.5 6.0 %copy-start.22 = (f32[64,128]{0,1:T(8,128)S(1)}, f32[64,128]{0,1:T(8,128)}, u32[]{:S(2)}) copy-start(f32[64,128]{0,1:T(8,128)} %copy.243) | copy-start | bytes 98308
  420.2 3.6 copy-start.18
  423.8 6.2 %copy-start.28 = (f32[3,1024]{1,0:T(4,128)S(1)}, f32[3,1024]{1,0:T(4,128)}, u32[]{:S(2)}) copy-start(f32[3,1024]{1,0:T(4,128)} %copy-done.27) | copy-start | bytes 36868
  423.9 6.2 %copy-start.30 = (f32[3,1024]{1,0:T(4,128)S(1)}, f32[3,1024]{1,0:T(4,128)}, u32[]{:S(2)}) copy-start(f32[3,1024]{1,0:T(4,128)} %copy-done.29) | copy-start | bytes 36868
  423.9 6.2 %copy-start.32 = (f32[3,1024]{1,0:T(4,128)S(1)}, f32[3,1024]{1,0:T(4,128)}, u32[]{:S(2)}) copy-start(f32[3,1024]{1,0:T(4,128)} %copy-done.31) | copy-start | bytes 36868
  423.9 6.2 %copy-start.34 = (f32[3,1024]{1,0:T(4,128)S(1)}, f32[3,1024]{1,0:T(4,128)}, u32[]{:S(2)}) copy-start(f32[3,1024]{1,0:T(4,128)} %copy-done.33) | copy-start | bytes 36868
  423.9 6.2 %copy-start.36 = (f32[3,1024]{1,0:T(4,128)S(1)}, f32[3,1024]{1,0:T(4,128)}, u32[]{:S(2)}) copy-start(f32[3,1024]{1,0:T(4,128)} %copy-done.35) | copy-start | bytes 36868
  423.9 6.2 %copy-start.38 = (f32[1,3,1024]{2,1,0:T(4,128)S(1)}, f32[1,3,1024]{2,1,0:T(4,128)}, u32[]{:S(2)}) copy-start(f32[1,3,1024]{2,1,0:T(4,128)} %copy-done.37) | copy-start | bytes 36868
  424.0 6.0 %collective-permute-start.1 = (bf16[3,1024,6]{1,2,0:T(8,128)(2,1)S(1)}, bf16[3,1024,6]{1,2,0:T(8,128)(2,1)S(1)}, u32[]{:S(2)}, u32[]{:S(2)}) collective-permute-start(bf16[3,1024,6]{1,2,0:T(8,128)(2,1)S(1)} %slice.120), channel_id=1, source_target_pairs={{4,0},{8,4},{12,8},{16,12},{20,16},{24,20},{28,24},{32,28},{36,32}... | collective-permute-start | bytes 110600 | tf_op jit(solution)/shard_map/ppermute | solution.py:17
  (5 other events, 8.3 us)
Sparse Core Ops, SparseCore 0:
  9.7 23.3 all-gather.4
  34.7 169.6 all-gather.2
  420.3 33.0 reduce-scatter.1
where the time goes:
time: 469 us; the launch traced here: 462 us
  waiting for transfers between devices  212 us (45%)
  matrix products  134 us (29%)
  local copies, waits for them, and re-layouts  55.9 us (12%)
  starting transfers between devices  31.5 us (7%)
  between operations  15.1 us (3%)
  other arithmetic  13.4 us (3%)
    all_gather x1, waiting for transfers between devices, local(): weight_full = lax.all_gather(out_weight, 'ctx', axis=1, tiled=True)  166 us
    reduce_scatter x1, waiting for transfers between devices, local(): lax.psum_scatter(lax.dot_general(weight_cols, gated_out, (((0,), (0,)), (...  20.6 us
    all_to_all x2, starting transfers between devices, to_owners(): lax.all_to_all(values_in.reshape(ctx_size, channels // ctx_size, 1, token...  18.2 us
    dot_general x6, matrix products, long_dft(): jnp.einsum('...pm,pl->...lm', part_re, cos_a, precision=precise)  16.4 us
    dot_general x6, matrix products, long_dft(): jnp.einsum('...pm,pl->...lm', part_re, sin_a, precision=precise)  14.7 us
    dot_general x6, matrix products, long_dft(): jnp.einsum('...pm,pl->...lm', part_im, sin_a, precision=precise)  14 us
    dot_general x6, matrix products, long_dft(): jnp.einsum('...lm,mk->...kl', z_re, cos_b, precision=precise)  13.6 us
    dot_general x6, matrix products, long_dft(): jnp.einsum('...lm,mk->...kl', z_re, sin_b, precision=precise)  13.6 us
  transfers between devices with their start and end apart: 9, of which 7 were waited for; matrix products, arithmetic and copies ran while one was open for 6% of the time, Pallas kernels for 0%

commit v1 on v0

v1 whole, which is shorter than its diff:
```python
import functools
import math

import jax
import jax.numpy as jnp
from jax import lax
from jax.experimental import pallas as pl
from jax.experimental.pallas import tpu as pltpu
from jax.sharding import PartitionSpec as P


def from_behind(block, axis, distance):
    devices = range(lax.axis_size(axis))
    route = [(i - distance, i) for i in devices if i - distance in devices]
    return lax.ppermute(block, axis, route)


def rims(edge_rows, step_by):
    return from_behind(edge_rows, "ctx", step_by)


def short_forward(projected, prev_rim, conv_weight):
    kernel = conv_weight.shape[0]
    tokens = projected.shape[2]
    extended = jnp.concatenate([prev_rim, projected], axis=2)
    summed = jnp.zeros(projected.shape, jnp.float32)
    for offset in range(kernel):
        begin_at = kernel - 1 - offset
        summed = summed + conv_weight[offset][:, :, None] * extended[
            :, :, begin_at : begin_at + tokens
        ].astype(jnp.float32)
    return summed.astype(jnp.bfloat16)


def short_backward(dshort, next_rim, conv_weight):
    kernel = conv_weight.shape[0]
    tokens = dshort.shape[2]
    extended = jnp.concatenate([dshort, next_rim], axis=2)
    summed = jnp.zeros(dshort.shape, jnp.float32)
    for offset in range(kernel):
        summed = summed + conv_weight[offset][:, :, None] * extended[
            :, :, offset : offset + tokens
        ].astype(jnp.float32)
    return summed.astype(jnp.bfloat16)


def to_owners(values_in, ctx_size):
    channels, tokens = values_in.shape
    return lax.all_to_all(
        values_in.reshape(ctx_size, channels // ctx_size, tokens), "ctx", split_axis=0, concat_axis=0, tiled=True
    )


def to_tokens(values_in):
    ctx_size, own_width, tokens = values_in.shape
    arrived = lax.all_to_all(values_in, "ctx", split_axis=0, concat_axis=0, tiled=True)
    return arrived.reshape(ctx_size * own_width, tokens)


BF, F32 = jnp.bfloat16, jnp.float32
NB = 32
OWN = 32
G = 2
T = 128

def dot(a, b, ca, cb):
    return lax.dot_general(a, b, (((ca,), (cb,)), ((), ())), preferred_element_type=F32)

def build_toeplitz(h_ref, hpad, M):
    for g in range(G):
        hpad[g:g + 1, 0:128] = jnp.zeros((1, 128), F32)
        hpad[g:g + 1, 128:] = h_ref[g:g + 1, :]
        M[g, 128:256, 0:128] = jnp.zeros((128, 128), BF)
    def step(e, c):
        for g in range(G):
            seg = hpad[g:g + 1, pl.ds(pl.multiple_of(e * 128, 128), 256)]
            tile = pltpu.roll(jnp.broadcast_to(seg, (128, 256)), 0, 1, stride=1, stride_axis=0)[:, 128:].astype(BF)
            M[g, 0:128, pl.ds(pl.multiple_of(e * 128, 128), 128)] = tile
            M[g, 128:256, pl.ds(pl.multiple_of(e * 128 + 128, 128), 128)] = tile
        return c
    lax.fori_loop(0, NB, step, 0)

def load_pairs(own, X, row0):
    for g in range(G):
        for h in range(2):
            v = own[...].reshape(NB // 2, 2, OWN, T)[:, h, 16 * g:16 * g + 16, :]
            X[g, row0:row0 + 256, T * h:T * h + T] = v.reshape(256, T)

def store_pairs(y, out, g):
    for j in range(NB // 2):
        for h in range(2):
            out[2 * j + h, 16 * g:16 * g + 16, :] = y[16 * j:16 * j + 16, T * h:T * h + T].astype(out.dtype)

def conv_forward(X, M, skip_rows, out):
    for g in range(G):
        acc = jnp.zeros((256, 256), F32)
        for d in range(16):
            acc = acc + dot(X[g, 256 - 16 * d:512 - 16 * d, :], M[g, :, 256 * d:256 * d + 256], 1, 0)
        y = acc + skip_rows(g) * X[g, 256:512, :].astype(F32)
        store_pairs(y, out, g)

def conv_backward(D, M, skip_rows, out):
    for g in range(G):
        acc = jnp.zeros((256, 256), F32)
        for d in range(16):
            acc = acc + dot(D[g, 16 * d:16 * d + 256, :], M[g, :, 256 * d:256 * d + 256], 1, 1)
        y = acc + skip_rows(g) * D[g, 0:256, :].astype(F32)
        store_pairs(y, out, g)

def filter_gradient(X, D, XR, carry, gacc, out, scaling):
    rows = lax.broadcasted_iota(jnp.int32, (256, 256), 0)
    cols = lax.broadcasted_iota(jnp.int32, (256, 256), 1)
    flip = jnp.where(rows + cols == 255, 1.0, 0.0).astype(BF)
    for g in range(G):
        XR[g] = dot(flip, X[g, 256:512, :], 1, 1).astype(BF)
    gacc[...] = jnp.zeros(gacc.shape, F32)
    carry[...] = jnp.zeros(carry.shape, F32)
    def shear(tile):
        wide = jnp.concatenate([tile, jnp.zeros((128, 128), F32)], axis=1)
        return jnp.sum(pltpu.roll(wide, 1, 1, stride=1, stride_axis=0), axis=0, keepdims=True)
    def step(d, c):
        for g in range(G):
            p = dot(XR[g], D[g, pl.ds(pl.multiple_of(16 * d, 16), 256), :], 1, 0)
            at = pl.multiple_of(256 * d, 128)
            gacc[g:g + 1, pl.ds(at, 256)] += shear(p[0:128, 0:128] + carry[g])
            at = pl.multiple_of(256 * d + 128, 128)
            gacc[g:g + 1, pl.ds(at, 256)] += shear(p[0:128, 128:] + p[128:, 0:128])
            carry[g] = p[128:, 128:]
        return c
    lax.fori_loop(0, 16, step, 0)
    for g in range(G):
        last = shear(carry[g])
        gacc[g:g + 1, 4096:4352] += last
        out[g:g + 1, :] = gacc[g:g + 1, 256:4352] * scaling

def skip_of(skip_ref):
    def rows(g):
        s = skip_ref[16 * g:16 * g + 16, :]
        return jnp.broadcast_to(s[None], (16, 16, 256)).reshape(256, 256)
    return rows

SCALE = 1.0 / math.sqrt(16 * 4096)

def kf(own, h, skip, out, hpad, M, X):
    build_toeplitz(h, hpad, M)
    X[:, 0:256, :] = jnp.zeros((G, 256, 256), BF)
    load_pairs(own, X, 256)
    conv_forward(X, M, skip_of(skip), out)

def kb(own, down, h, skip, out, fg, hpad, M, X, D, XR, carry, gacc):
    build_toeplitz(h, hpad, M)
    load_pairs(own, X, 256)
    D[:, 256:512, :] = jnp.zeros((G, 256, 256), BF)
    load_pairs(down, D, 0)
    conv_backward(D, M, skip_of(skip), out)
    filter_gradient(X, D, XR, carry, gacc, fg, SCALE)

HP = pltpu.VMEM((G, 4096 + 128), F32)
MS = pltpu.VMEM((G, 256, 4096 + 128), BF)
XS = pltpu.VMEM((G, 512, 256), BF)

def long_forward(own, h, skip):
    return pl.pallas_call(kf, out_shape=jax.ShapeDtypeStruct((NB, OWN, T), BF),
        scratch_shapes=[HP, MS, XS], compiler_params=pltpu.CompilerParams(vmem_limit_bytes=40 << 20), name="long_forward")(own, h, skip)

def long_backward(own, down, h, skip):
    return pl.pallas_call(kb, out_shape=(jax.ShapeDtypeStruct((NB, OWN, T), BF), jax.ShapeDtypeStruct((G, 4096), F32)),
        scratch_shapes=[HP, MS, XS, XS, pltpu.VMEM((G, 256, 256), BF), pltpu.VMEM((G, 128, 128), F32), pltpu.VMEM((G, 4352), F32)],
        compiler_params=pltpu.CompilerParams(vmem_limit_bytes=40 << 20), name="long_backward")(own, down, h, skip)


def local(projected, conv_weight, filters, skip_gain, out_weight, cotangent):
    kernel = conv_weight.shape[0]
    channels = projected.shape[1]
    tokens = projected.shape[2]
    ctx_size = lax.axis_size("ctx")
    own_width = channels // ctx_size
    weight_full = lax.all_gather(out_weight, "ctx", axis=1, tiled=True)
    prev_rim = rims(projected[:, :, tokens - (kernel - 1) :], 1)
    short_out = short_forward(projected, prev_rim, conv_weight)
    mix_input = (short_out[1].astype(jnp.float32) * short_out[2].astype(jnp.float32)).astype(
        jnp.bfloat16
    )
    weight_cols = weight_full
    dgated = jnp.dot(
        weight_cols,
        lax.all_gather(cotangent, "tp", axis=0, tiled=True),
        preferred_element_type=jnp.float32,
    ).astype(jnp.bfloat16)
    dlongmix = (dgated.astype(jnp.float32) * short_out[0].astype(jnp.float32)).astype(jnp.bfloat16)
    skip_own = lax.dynamic_slice_in_dim(skip_gain, lax.axis_index("ctx") * own_width, own_width)
    own_taps = filters[0]
    mix_own = to_owners(mix_input, ctx_size)
    skip_own = skip_own[:, None]
    long_own = long_forward(mix_own, own_taps, skip_own)
    longmix = to_tokens(long_own)
    dlong_own = to_owners(dlongmix, ctx_size)
    dmix_own, filter_grad = long_backward(mix_own, dlong_own, own_taps, skip_own)
    filter_grad = filter_grad[None]
    dmix_input = to_tokens(dmix_own)
    gated_out = (short_out[0].astype(jnp.float32) * longmix.astype(jnp.float32)).astype(
        jnp.bfloat16
    )
    weight_cols = weight_full
    block_out = lax.psum_scatter(
        lax.dot_general(
            weight_cols, gated_out, (((0,), (0,)), ((), ())), preferred_element_type=jnp.float32
        ).astype(jnp.bfloat16),
        "tp",
        scatter_dimension=0,
        tiled=True,
    )
    dmix_vals = dmix_input.astype(jnp.float32)
    dshort = jnp.stack(
        [
            dgated.astype(jnp.float32) * longmix.astype(jnp.float32),
            dmix_vals * short_out[2].astype(jnp.float32),
            dmix_vals * short_out[1].astype(jnp.float32),
        ]
    ).astype(jnp.bfloat16)
    next_rim = rims(dshort[:, :, : kernel - 1], -1)
    proj_grad = short_backward(dshort, next_rim, conv_weight)
    return (block_out, proj_grad, filter_grad)


def solution(mesh):
    return jax.shard_map(
        local,
        mesh=mesh,
        in_specs=(
            P(None, "tp", "ctx"),
            P(None, None, "tp"),
            P("tp", "ctx", None),
            P("tp"),
            P("tp", "ctx"),
            P("tp", "ctx"),
        ),
        out_specs=(P("tp", "ctx"), P(None, "tp", "ctx"), P("tp", "ctx", None)),
        check_vma=False,
    )
```

time: 469 us -> 278 us (0.59); the launches traced: 462 us -> 277 us
  matrix products: 134 us -> 12.2 us
  local copies, waits for them, and re-layouts: 55.9 us -> 6.06 us
  waiting for transfers between devices: 212 us -> 168 us
  blocking collectives: 0 us -> 43.6 us
  starting transfers between devices: 31.5 us -> 14.9 us
  Pallas kernels: 0 us -> 15.7 us
  other arithmetic: 13.4 us -> 3.34 us
    dot_general x60 -> x0, matrix products: 121 us -> none  [the longest x6 16.4 us: long_dft(): jnp.einsum('...pm,pl->...lm', part_re, cos_a, precision=precise)]
    all_to_all x0 -> x3, blocking collectives: none -> 43.6 us  [the longest x2 26.9 us: to_tokens(): lax.all_to_all(values_in, 'ctx', split_axis=0, concat_axis=0, tiled=True)]
    all_gather x1, waiting for transfers between devices: 166 us -> 134 us  [local(): weight_full = lax.all_gather(out_weight, 'ctx', axis=1, tiled=True)]
    reduce_scatter x1, waiting for transfers between devices: 20.6 us -> 0.01 us  [local(): lax.psum_scatter(lax.dot_general(weight_cols, gated_out, (((0,), (0,)), (...]
    all_gather x1, waiting for transfers between devices: 0.02 us -> 17.3 us  [local(): lax.all_gather(cotangent, 'tp', axis=0, tiled=True)]
    all_to_all x4 -> x1, starting transfers between devices: 26.2 us -> 9.6 us  [to_owners(): lax.all_to_all(values_in.reshape(ctx_size, channels // ctx_size, tokens),...]
    pallas_call x0 -> x2, Pallas kernels: none -> 15.7 us  [the longest x1 10.8 us: long_backward(): pl.pallas_call(kb, out_shape=(jax.ShapeDtypeStruct((NB, OWN, T), BF), jax...]
    sub x9 -> x0, local copies, waits for them, and re-layouts: 15.4 us -> none  [the longest x5 7.82 us: long_dft(): jnp.einsum('...lm,mk->...kl', z_re, cos_b, precision=precise)]
  transfers between devices with their start and end apart: 9 -> 6, of which waited for: 7 -> 5; matrix products, arithmetic and copies ran while one was open for 6% -> 7% of each run, Pallas kernels for 0% -> 6%
where the time goes in v1:
time: 278 us; the launch traced here: 277 us
  waiting for transfers between devices  168 us (60%)
  blocking collectives  43.6 us (16%)
  Pallas kernels  15.7 us (6%)
  starting transfers between devices  14.9 us (5%)
  between operations  14 us (5%)
  matrix products  12.2 us (4%)
  local copies, waits for them, and re-layouts  6.06 us (2%)
  other arithmetic  3.34 us (1%)
    all_gather x1, waiting for transfers between devices, local(): weight_full = lax.all_gather(out_weight, 'ctx', axis=1, tiled=True)  134 us
    all_to_all x2, blocking collectives, to_tokens(): lax.all_to_all(values_in, 'ctx', split_axis=0, concat_axis=0, tiled=True)  26.9 us
    all_gather x1, waiting for transfers between devices, local(): lax.all_gather(cotangent, 'tp', axis=0, tiled=True)  17.3 us
    all_to_all x1, blocking collectives, to_owners(): lax.all_to_all(values_in.reshape(ctx_size, channels // ctx_size, tokens),...  16.7 us
    pallas_call x1, Pallas kernels, long_backward(): pl.pallas_call(kb, out_shape=(jax.ShapeDtypeStruct((NB, OWN, T), BF), jax...  10.8 us
    all_to_all x1, starting transfers between devices, to_owners(): lax.all_to_all(values_in.reshape(ctx_size, channels // ctx_size, tokens),...  9.6 us
    all_to_all x1, waiting for transfers between devices, to_owners(): lax.all_to_all(values_in.reshape(ctx_size, channels // ctx_size, tokens),...  9.25 us
    dot_general x1, matrix products, local(): jnp.dot(weight_cols, lax.all_gather(cotangent, 'tp', axis=0, tiled=True),...  6.51 us
  transfers between devices with their start and end apart: 6, of which 5 were waited for; matrix products, arithmetic and copies ran while one was open for 7% of the time, Pallas kernels for 6%

profile of v1, /device:TPU:0, one launch (start us, length us, event | category | flops | bytes accessed | tf_op | source)
XLA Modules:
  0.0 277.3 jit_solution(3242688568085386886)
XLA Ops:
  7.2 0.0 copy-start
  7.2 0.0 copy-start.2
  7.2 0.0 all-gather.3.cloned.1.call-start
  7.2 0.7 all-gather.3.cloned.1.call-update
  7.9 0.0 all-gather.5.cloned.1.call-start
  8.0 1.4 copy.22
  9.4 3.9 %collective-permute-start = (bf16[3,1024,6]{1,2,0:T(8,128)(2,1)S(1)}, bf16[3,1024,6]{1,2,0:T(8,128)(2,1)S(1)}, u32[]{:S(2)}, u32[]{:S(2)}) collective-permute-start(bf16[3,1024,6]{1,2,0:T(8,128)(2,1)S(1)} %slice.106), channel_id=1, source_target_pairs={{0,4},{4,8},{8,12},{12,16},{16,20},{20,24},{24,28},{28,32},{32,36}... | collective-permute-start | bytes 110600 | tf_op jit(solution)/shard_map/ppermute | solution.py:15
  13.3 0.0 all-gather.5.cloned.1.call-update
  13.3 0.0 copy-done.2
  13.4 0.1 fusion.14
  13.5 1.6 collective-permute-done
  15.1 0.0 copy-start.1
  15.1 1.5 add_convert_fusion.1
  16.6 0.1 fusion.8
  16.6 0.8 copy.25
  17.5 9.6 %all-to-all-start = ((bf16[32,32,128]{2,1,0:T(8,128)(2,1)}), bf16[32,32,128]{2,1,0:T(8,128)(2,1)S(1)}, u32[]{:S(2)}, u32[]{:S(2)}) async-start(bf16[32,32,128]{2,1,0:T(8,128)(2,1)} %bitcast.1), calls=%async_computation | async-start | bytes 524288 | tf_op jit(solution)/shard_map/all_to_all | solution.py:49
  27.1 0.0 reduce-scatter.2.cloned.1.call-start
  27.1 0.0 copy-done
  27.1 0.1 dynamic-slice_bitcast_fusion
  27.2 0.1 copy.26.skip
  27.3 9.3 %all-to-all-done.own = bf16[32,32,128]{2,1,0:T(8,128)(2,1)S(1)} async-done(((bf16[32,32,128]{2,1,0:T(8,128)(2,1)}), bf16[32,32,128]{2,1,0:T(8,128)(2,1)S(1)}, u32[]{:S(2)}, u32[]{:S(2)}) %all-to-all-start) | async-done | bytes 262176 | tf_op jit(solution)/shard_map/all_to_all | solution.py:49
  36.6 0.0 copy-done.1
  36.6 4.9 %long_forward.1 = bf16[32,32,128]{2,1,0:T(8,128)(2,1)S(1)} custom-call(bf16[32,32,128]{2,1,0:T(8,128)(2,1)S(1)} %all-to-all-done.own, f32[2,4096]{1,0:T(2,128)S(1)} %bitcast.43, f32[32,1]{1,0:T(8,128)S(1)} %copy.26.skip), custom_call_target="tpu_custom_call" | custom-call | tf_op jit(solution)/shard_map/long_forward/pallas_call | solution.py:163
  41.4 14.2 %all_to_all.20 = bf16[32,32,128]{2,1,0:T(8,128)(2,1)S(1)} all-to-all(bf16[32,32,128]{2,1,0:T(8,128)(2,1)S(1)} %long_forward.1), channel_id=1, replica_groups=mesh['ctx'=32,'tp'=4] {'ctx'}, dimensions={0} | all-to-all | bytes 524288 | tf_op jit(solution)/shard_map/all_to_all | solution.py:56
  55.6 0.1 bitcast_convert_fusion.1
  55.6 0.2 copy.27
  55.9 134.0 %all-gather.3.cloned.1.call-done = bf16[1024,4096]{1,0:T(8,128)(2,1)} async-done(((bf16[1024,128]{1,0:T(8,128)(2,1)}), bf16[1024,4096]{1,0:T(8,128)(2,1)}) %all-gather.3.cloned.1.call-update) | async-done | bytes 8388624 | tf_op jit(solution)/shard_map/all_gather | solution.py:178
  189.9 5.7 %fusion = bf16[4096,128]{0,1:T(8,128)(2,1)} fusion(bf16[1024,4096]{1,0:T(8,128)(2,1)} %all-gather.3.cloned.1.call-done, f32[1024,128]{0,1:T(8,128)S(1)} %copy.27, bf16[3,1024,128]{1,2,0:T(8,128)(2,1)S(1)} %add_convert_fusion.1), kind=kOutput, calls=%fused_computation.1 | convolution fusion | flops 1074659328 | bytes 10223616 | tf_op jit(solution)/shard_map/dot_general | solution.py:206
  195.5 0.0 reduce-scatter.2.cloned.1.call-update
  195.6 17.3 %all-gather.5.cloned.1.call-done = bf16[4096,128]{1,0:T(8,128)(2,1)} async-done(((bf16[1024,128]{1,0:T(8,128)(2,1)}), bf16[4096,128]{1,0:T(8,128)(2,1)}) %all-gather.5.cloned.1.call-update) | async-done | bytes 1048592 | tf_op jit(solution)/shard_map/all_gather | solution.py:187
  212.9 6.5 %fusion.12 = (bf16[1,1024,128]{1,2,0:T(8,128)(2,1)S(1)}, bf16[1024,128]{0,1:T(8,128)(2,1)S(1)}) fusion(f32[1024,128]{0,1:T(8,128)S(1)} %copy.27, bf16[3,1024,128]{1,2,0:T(8,128)(2,1)S(1)} %add_convert_fusion.1, bf16[1024,4096]{1,0:T(8,128)(2,1)} %all-gather.3.cloned.1.call-done, bf16[4096,128]{1,0:T(8,128)(2,1)} %all-gather.5.cloned.1.call-done), kind=kOutput, calls=%fused_computation.33 | convolution fusion | flops 1074659328 | bytes 10747904 | tf_op jit(solution)/shard_map/dot_general | solution.py:185
  219.4 0.2 copy.29
  219.6 16.7 %all_to_all.21.down = bf16[32,32,128]{2,1,0:T(8,128)(2,1)S(1)} all-to-all(bf16[32,32,128]{2,1,0:T(8,128)(2,1)S(1)} %bitcast.46), channel_id=1, replica_groups=mesh['ctx'=32,'tp'=4] {'ctx'}, dimensions={0} | all-to-all | bytes 524288 | tf_op jit(solution)/shard_map/all_to_all | solution.py:49
  236.3 10.8 %long_backward.1 = (bf16[32,32,128]{2,1,0:T(8,128)(2,1)S(1)}, f32[2,4096]{1,0:T(2,128)}) custom-call(bf16[32,32,128]{2,1,0:T(8,128)(2,1)S(1)} %all-to-all-done.own, bf16[32,32,128]{2,1,0:T(8,128)(2,1)S(1)} %all_to_all.21.down, f32[2,4096]{1,0:T(2,128)S(1)} %bitcast.44, f32[32,1]{1,0:T(8,128)S(1)} %copy.26.skip), custom_call_target="tpu_custom_call" | custom-call | tf_op jit(solution)/shard_map/long_backward/pallas_call | solution.py:167
  247.1 12.8 %all_to_all.22 = bf16[32,32,128]{2,1,0:T(8,128)(2,1)S(1)} all-to-all(bf16[32,32,128]{2,1,0:T(8,128)(2,1)S(1)} %get-tuple-element.5), channel_id=1, replica_groups=mesh['ctx'=32,'tp'=4] {'ctx'}, dimensions={0} | all-to-all | bytes 524288 | tf_op jit(solution)/shard_map/all_to_all | solution.py:56
  259.9 0.2 copy.31
  260.1 0.1 fusion.9
  260.2 0.1 pad_maximum_fusion.2
  260.3 1.3 collective-permute-start.1
  261.6 4.7 %collective-permute-done.1 = bf16[3,1024,6]{1,2,0:T(8,128)(2,1)S(1)} collective-permute-done((bf16[3,1024,6]{1,2,0:T(8,128)(2,1)S(1)}, bf16[3,1024,6]{1,2,0:T(8,128)(2,1)S(1)}, u32[]{:S(2)}, u32[]{:S(2)}) %collective-permute-start.1) | collective-permute-done | bytes 36896 | tf_op jit(solution)/shard_map/ppermute | solution.py:15
  266.3 0.1 pad_maximum_fusion
  266.4 1.4 add_convert_fusion
  267.8 1.2 copy.34
  269.0 0.0 reduce-scatter.2.cloned.1.call-done
  269.0 1.8 copy.33
  (7 shorter events, 0.1 us)
Async XLA Ops:
  7.2 20.0 %copy-start = (f32[1024]{0:T(1024)S(1)}, f32[1024]{0:T(1024)}, u32[]{:S(2)}) copy-start(f32[1024]{0:T(1024)} %param.9) | copy-start | bytes 12292
  7.2 6.2 %copy-start.2 = (f32[7,3,1024]{2,0,1:T(8,128)S(1)}, f32[7,3,1024]{2,0,1:T(8,128)}, u32[]{:S(2)}) copy-start(f32[7,3,1024]{2,0,1:T(8,128)} %param.7) | copy-start | bytes 258052
  7.2 182.7 %all-gather.3.cloned.1.call-start = ((), (), s32[]{:S(2)}) async-start(), calls=%async_computation.5 | async-start | bytes 8650752 | tf_op jit(solution)/shard_map/all_gather | solution.py:178
  7.9 205.0 %all-gather.5.cloned.1.call-start = ((), (), s32[]{:S(2)}) async-start(), calls=%async_computation.7 | async-start | bytes 1310720 | tf_op jit(solution)/shard_map/all_gather | solution.py:187
  9.4 5.6 %collective-permute-start = (bf16[3,1024,6]{1,2,0:T(8,128)(2,1)S(1)}, bf16[3,1024,6]{1,2,0:T(8,128)(2,1)S(1)}, u32[]{:S(2)}, u32[]{:S(2)}) collective-permute-start(bf16[3,1024,6]{1,2,0:T(8,128)(2,1)S(1)} %slice.106), channel_id=1, source_target_pairs={{0,4},{4,8},{8,12},{12,16},{16,20},{20,24},{24,28},{28,32},{32,36}... | collective-permute-start | bytes 110600 | tf_op jit(solution)/shard_map/ppermute | solution.py:15
  15.1 21.5 %copy-start.1 = (f32[1,2,4096]{2,1,0:T(2,128)S(1)}, f32[1,2,4096]{2,1,0:T(2,128)}, u32[]{:S(2)}) copy-start(f32[1,2,4096]{2,1,0:T(2,128)} %param.8) | copy-start | bytes 98308
  17.5 19.1 %all-to-all-start = ((bf16[32,32,128]{2,1,0:T(8,128)(2,1)}), bf16[32,32,128]{2,1,0:T(8,128)(2,1)S(1)}, u32[]{:S(2)}, u32[]{:S(2)}) async-start(bf16[32,32,128]{2,1,0:T(8,128)(2,1)} %bitcast.1), calls=%async_computation | async-start | bytes 524288 | tf_op jit(solution)/shard_map/all_to_all | solution.py:49
  27.1 241.9 %reduce-scatter.2.cloned.1.call-start = ((), (), s32[]{:S(2)}) async-start(), calls=%async_computation.6 | async-start | bytes 1310720 | tf_op jit(solution)/shard_map/reduce_scatter | solution.py:205
  260.3 6.0 %collective-permute-start.1 = (bf16[3,1024,6]{1,2,0:T(8,128)(2,1)S(1)}, bf16[3,1024,6]{1,2,0:T(8,128)(2,1)S(1)}, u32[]{:S(2)}, u32[]{:S(2)}) collective-permute-start(bf16[3,1024,6]{1,2,0:T(8,128)(2,1)S(1)} %slice.120), channel_id=1, source_target_pairs={{4,0},{8,4},{12,8},{16,12},{20,16},{24,20},{28,24},{32,28},{36,32}... | collective-permute-start | bytes 110600 | tf_op jit(solution)/shard_map/ppermute | solution.py:15
Sparse Core Ops, SparseCore 0:
  9.6 180.2 all-gather.2
  191.5 21.3 all-gather.4
  215.5 31.2 reduce-scatter.1

commit v2 on v1

--- a/solution.py
+++ b/solution.py
@@ -42,19 +42,6 @@
             :, :, offset : offset + tokens
         ].astype(jnp.float32)
     return summed.astype(jnp.bfloat16)
-
-
-def to_owners(values_in, ctx_size):
-    channels, tokens = values_in.shape
-    return lax.all_to_all(
-        values_in.reshape(ctx_size, channels // ctx_size, tokens), "ctx", split_axis=0, concat_axis=0, tiled=True
-    )
-
-
-def to_tokens(values_in):
-    ctx_size, own_width, tokens = values_in.shape
-    arrived = lax.all_to_all(values_in, "ctx", split_axis=0, concat_axis=0, tiled=True)
-    return arrived.reshape(ctx_size * own_width, tokens)
 
 
 BF, F32 = jnp.bfloat16, jnp.float32
@@ -169,47 +156,224 @@
         compiler_params=pltpu.CompilerParams(vmem_limit_bytes=40 << 20), name="long_backward")(own, down, h, skip)
 
 
+MESH = pl.DeviceIdType.MESH
+
+def ring_barrier(me):
+    sem = pltpu.get_barrier_semaphore()
+
+    def one(k, c):
+        pl.semaphore_signal(sem, inc=1, device_id=((me.ctx + k) % 32, me.tp), device_id_type=MESH)
+        return c
+
+    lax.fori_loop(1, 32, one, 0)
+    pl.semaphore_wait(sem, 31)
+
+
+def group_barrier(me):
+    sem = pltpu.get_barrier_semaphore()
+    for same in (1, 0):
+        for k in range(same, 4):
+            dev = (me.ctx if same else me.partner, (me.tp + k) % 4)
+            pl.semaphore_signal(sem, inc=1, device_id=dev, device_id_type=MESH)
+    pl.semaphore_wait(sem, 7)
+
+
+def plane_barrier(me):
+    sem = pltpu.get_barrier_semaphore()
+    for dx, dz in ((1, 0), (3, 0), (0, 1), (0, 3)):
+        dev = (me.at((me.x + dx) % 4, (me.z + dz) % 4), me.tp)
+        pl.semaphore_signal(sem, inc=1, device_id=dev, device_id_type=MESH)
+    pl.semaphore_wait(sem, 4)
+
+
+class Place:
+    def __init__(self):
+        self.ctx = lax.axis_index("ctx"); self.tp = lax.axis_index("tp")
+        self.x = self.ctx // 8; self.lo = (self.ctx // 4) % 2; self.z = self.ctx % 4
+        self.partner = self.ctx + 4 - 8 * self.lo
+    def at(self, x, z):
+        return x * 8 + self.lo * 4 + z
+
+def relay(me, w_ref, wg, ssem, rsem):
+    x, z = me.x, me.z
+    k = [0]
+    sends = []
+    def send(src, dst, dev):
+        c = pltpu.make_async_remote_copy(src_ref=src, dst_ref=dst, send_sem=ssem.at[k[0]], recv_sem=rsem.at[k[0]],
+                                         device_id=(dev, me.tp), device_id_type=MESH)
+        c.start(); k[0] += 1
+        sends.append(c)
+        return c
+    def geometry(h):
+        if h == 0:
+            slot = lambda f, s: ((x + s) % 4) * 4 + (z + f) % 4
+            dev = lambda f, s: me.at((x + s) % 4, (z + f) % 4)
+        else:
+            slot = lambda f, s: ((x + f) % 4) * 4 + (z + s) % 4
+            dev = lambda f, s: me.at((x + f) % 4, (z + s) % 4)
+        return slot, dev, 512 * h
+    halves = [geometry(0), geometry(1)]
+    def part(ref, slot, r0, n):
+        return ref.at[slot, pl.ds(r0, n), :]
+    first, second = [None, None], [{}, {}]
+    for h in (0, 1):
+        slot, dev, r = halves[h]
+        src = w_ref.at[pl.ds(r, 512), :]
+        first[h] = [send(src, part(wg, slot(0, 0), r, 512), dev(1, 0)), send(src, part(wg, slot(0, 0), r, 512), dev(-1, 0))]
+    for h in (0, 1):
+        slot, dev, r = halves[h]
+        src = w_ref.at[pl.ds(r, 512), :]
+        second[h][0] = [send(src, part(wg, slot(0, 0), r, 512), dev(0, 1)), send(src, part(wg, slot(0, 0), r, 512), dev(0, -1))]
+    fwd = [[None, None], [None, None]]
+    for i, f in ((0, -1), (1, 1)):
+        for h in (0, 1):
+            slot, dev, r = halves[h]
+            first[h][i].wait_recv()
+            b = slot(f, 0)
+            rr = r + 256 * i
+            fwd[h][i] = send(part(wg, b, rr, 256), part(wg, b, rr, 256), dev(-f, 0))
+            second[h][f] = [send(part(wg, b, r, 512), part(wg, b, r, 512), dev(0, 1)), send(part(wg, b, r, 512), part(wg, b, r, 512), dev(0, -1))]
+    last = []
+    def forward2(h, f):
+        slot, dev, r = halves[h]
+        for i, s in ((0, -1), (1, 1)):
+            second[h][f][i].wait_recv()
+            b = slot(f, s)
+            rr = r + 256 * i
+            last.append(send(part(wg, b, rr, 256), part(wg, b, rr, 256), dev(0, -s)))
+    for h in (0, 1):
+        forward2(h, 0)
+    for h in (0, 1):
+        slot, dev, r = halves[h]
+        for i in (0, 1):
+            fwd[h][i].wait_recv()
+        b = slot(2, 0)
+        second[h][2] = [send(part(wg, b, r, 512), part(wg, b, r, 512), dev(0, 1)), send(part(wg, b, r, 512), part(wg, b, r, 512), dev(0, -1))]
+    for f in (-1, 1, 2):
+        for h in (0, 1):
+            forward2(h, f)
+    for c in last:
+        c.wait_recv()
+    return sends
+
+N_RELAY = 40
+
+def relay_kernel(w_ref, out, ssem, rsem, lsem):
+    me = Place()
+    own = pltpu.make_async_copy(w_ref, out.at[me.x * 4 + me.z], lsem)
+    own.start()
+    plane_barrier(me)
+    sends = relay(me, w_ref, out, ssem, rsem)
+    for c in sends: c.wait_send()
+    own.wait()
+
+def a2a_kernel(v_ref, out, ssem, rsem, lsem):
+    me = Place()
+    own = pltpu.make_async_copy(v_ref.at[me.ctx], out.at[me.ctx], lsem)
+    own.start()
+    ring_barrier(me)
+    def mk(k):
+        to = (me.ctx + k) % 32
+        return pltpu.make_async_remote_copy(src_ref=v_ref.at[to], dst_ref=out.at[me.ctx], send_sem=ssem.at[k], recv_sem=rsem.at[k],
+            device_id=(to, me.tp), device_id_type=MESH)
+    def go(k, c): mk(k).start(); return c
+    def wt(k, c): mk(k).wait(); return c
+    lax.fori_loop(1, 32, go, 0)
+    lax.fori_loop(1, 32, wt, 0)
+    own.wait()
+
+def ygroup_kernel(v_ref, out, ssem, rsem, lsem):
+    me = Place()
+    own = pltpu.make_async_copy(v_ref.at[pl.ds(512 * me.lo, 512), :], out.at[me.lo, pl.ds(512 * me.tp, 512), :], lsem)
+    own.start()
+    group_barrier(me)
+    cs = []
+    n = 0
+    for same in (1, 0):
+        for k in range(4):
+            if same and k == 0: continue
+            lo2 = me.lo if same else 1 - me.lo
+            ctx2 = me.ctx if same else me.partner
+            c = pltpu.make_async_remote_copy(src_ref=v_ref.at[pl.ds(512 * lo2, 512), :], dst_ref=out.at[me.lo, pl.ds(512 * me.tp, 512), :],
+              send_sem=ssem.at[n], recv_sem=rsem.at[n], device_id=(ctx2, (me.tp + k) % 4), device_id_type=MESH)
+            c.start(); cs.append(c); n += 1
+    for c in cs: c.wait()
+    own.wait()
+
+
+def spread_kernel(v_ref, out, ssem, rsem, lsem):
+    me = Place()
+    own = pltpu.make_async_copy(v_ref.at[me.lo, me.tp], out.at[me.lo, me.tp], lsem)
+    own.start()
+    group_barrier(me)
+    cs = []
+    for same in (1, 0):
+        for k in range(same, 4):
+            lo2 = me.lo if same else 1 - me.lo
+            tp2 = (me.tp + k) % 4
+            c = pltpu.make_async_remote_copy(
+                src_ref=v_ref.at[lo2, tp2], dst_ref=out.at[me.lo, me.tp], send_sem=ssem.at[len(cs)],
+                recv_sem=rsem.at[len(cs)], device_id=(me.ctx if same else me.partner, tp2), device_id_type=MESH)
+            c.start()
+            cs.append(c)
+    for c in cs:
+        c.wait()
+    own.wait()
+
+
+def call(kern, out, cid, sems, arg):
+    return pl.pallas_call(
+        kern, out_shape=jax.ShapeDtypeStruct(out, BF), in_specs=[pl.BlockSpec(memory_space=pltpu.VMEM)],
+        out_specs=pl.BlockSpec(memory_space=pltpu.VMEM), name=kern.__name__,
+        scratch_shapes=[pltpu.SemaphoreType.DMA((sems,)), pltpu.SemaphoreType.DMA((sems,)), pltpu.SemaphoreType.DMA],
+        compiler_params=pltpu.CompilerParams(collective_id=cid, has_side_effects=True, vmem_limit_bytes=32 << 20),
+    )(arg)
+
+
+def to_owners(values_in):
+    return call(a2a_kernel, (32, 32, 128), 3, 32, values_in.reshape(32, 32, 128))
+
+
+def to_tokens(values_in):
+    return call(a2a_kernel, (32, 32, 128), 3, 32, values_in).reshape(1024, 128)
+
+
+def swap(values_in):
+    return lax.ppermute(values_in, "ctx", [(i, i ^ 4) for i in range(32)])
+
+
 def local(projected, conv_weight, filters, skip_gain, out_weight, cotangent):
     kernel = conv_weight.shape[0]
     channels = projected.shape[1]
     tokens = projected.shape[2]
-    ctx_size = lax.axis_size("ctx")
-    own_width = channels // ctx_size
-    weight_full = lax.all_gather(out_weight, "ctx", axis=1, tiled=True)
+    own_width = OWN
+    ctx = lax.axis_index("ctx")
+    lo = (ctx // 4) % 2
+    weights = call(relay_kernel, (16, 1024, 128), 1, N_RELAY, out_weight)
+    cot = call(ygroup_kernel, (2, 2048, 128), 2, 8, cotangent)
     prev_rim = rims(projected[:, :, tokens - (kernel - 1) :], 1)
     short_out = short_forward(projected, prev_rim, conv_weight)
     mix_input = (short_out[1].astype(jnp.float32) * short_out[2].astype(jnp.float32)).astype(
         jnp.bfloat16
     )
-    weight_cols = weight_full
-    dgated = jnp.dot(
-        weight_cols,
-        lax.all_gather(cotangent, "tp", axis=0, tiled=True),
-        preferred_element_type=jnp.float32,
-    ).astype(jnp.bfloat16)
+    part = jnp.einsum("sco,bsot->bct", weights, cot.reshape(2, 16, 128, 128), preferred_element_type=F32)
+    mine = lax.dynamic_index_in_dim(part, lo, 0, False)
+    theirs = lax.dynamic_index_in_dim(part, 1 - lo, 0, False).astype(BF)
+    dgated = (mine + swap(theirs).astype(F32)).astype(BF)
     dlongmix = (dgated.astype(jnp.float32) * short_out[0].astype(jnp.float32)).astype(jnp.bfloat16)
-    skip_own = lax.dynamic_slice_in_dim(skip_gain, lax.axis_index("ctx") * own_width, own_width)
+    skip_own = lax.dynamic_slice_in_dim(skip_gain, ctx * own_width, own_width)[:, None]
     own_taps = filters[0]
-    mix_own = to_owners(mix_input, ctx_size)
-    skip_own = skip_own[:, None]
-    long_own = long_forward(mix_own, own_taps, skip_own)
-    longmix = to_tokens(long_own)
-    dlong_own = to_owners(dlongmix, ctx_size)
+    mix_own = to_owners(mix_input)
+    longmix = to_tokens(long_forward(mix_own, own_taps, skip_own))
+    dlong_own = to_owners(dlongmix)
     dmix_own, filter_grad = long_backward(mix_own, dlong_own, own_taps, skip_own)
-    filter_grad = filter_grad[None]
     dmix_input = to_tokens(dmix_own)
-    gated_out = (short_out[0].astype(jnp.float32) * longmix.astype(jnp.float32)).astype(
-        jnp.bfloat16
-    )
-    weight_cols = weight_full
-    block_out = lax.psum_scatter(
-        lax.dot_general(
-            weight_cols, gated_out, (((0,), (0,)), ((), ())), preferred_element_type=jnp.float32
-        ).astype(jnp.bfloat16),
-        "tp",
-        scatter_dimension=0,
-        tiled=True,
-    )
+    gated = (short_out[0].astype(jnp.float32) * longmix.astype(jnp.float32)).astype(jnp.bfloat16)
+    other = swap(gated)
+    both = jnp.stack([jnp.where(lo == 0, gated, other), jnp.where(lo == 0, other, gated)])
+    share = jnp.einsum("bct,pzco->bptzo", both, weights.reshape(4, 4, 1024, 128), preferred_element_type=F32)
+    shares = call(spread_kernel, (2, 4, 128, 512), 4, 8, share.astype(BF).reshape(2, 4, 128, 512))
+    block_out = jnp.sum(shares.astype(F32), axis=1).transpose(0, 2, 1).reshape(1024, 128).astype(BF)
     dmix_vals = dmix_input.astype(jnp.float32)
     dshort = jnp.stack(
         [
@@ -220,7 +384,7 @@
     ).astype(jnp.bfloat16)
     next_rim = rims(dshort[:, :, : kernel - 1], -1)
     proj_grad = short_backward(dshort, next_rim, conv_weight)
-    return (block_out, proj_grad, filter_grad)
+    return (block_out, proj_grad, filter_grad[None])
 
 
 def solution(mesh):

time: 278 us -> 158 us (0.57)
  waiting for transfers between devices: 168 us -> 0.06 us
  Pallas kernels: 15.7 us -> 119 us
  blocking collectives: 43.6 us -> 0 us
  between operations: 14 us -> 0.98 us
  other arithmetic: 3.34 us -> 12.4 us
  matrix products: 12.2 us -> 5.26 us
  starting transfers between devices: 14.9 us -> 11.2 us
    all_gather x2 -> x0, waiting for transfers between devices: 151 us -> none  [the longest x1 134 us: local(): weight_full = lax.all_gather(out_weight, 'ctx', axis=1, tiled=True)]
    pallas_call x0 -> x7, Pallas kernels: none -> 103 us  [call(): pl.pallas_call(kern, out_shape=jax.ShapeDtypeStruct(out, BF), in_specs=[p...]
    all_to_all x3 -> x0, blocking collectives: 43.6 us -> none  [the longest x2 26.9 us: to_tokens(): lax.all_to_all(values_in, 'ctx', split_axis=0, concat_axis=0, tiled=True)]
    all_to_all x1 -> x0, starting transfers between devices: 9.6 us -> none  [to_owners(): lax.all_to_all(values_in.reshape(ctx_size, channels // ctx_size, tokens),...]
    all_to_all x1 -> x0, waiting for transfers between devices: 9.25 us -> none  [to_owners(): lax.all_to_all(values_in.reshape(ctx_size, channels // ctx_size, tokens),...]
    dot_general x2, matrix products: 12.2 us -> 5.26 us  [the longest x1 3.47 us: local(): jnp.einsum('sco,bsot->bct', weights, cot.reshape(2, 16, 128, 128), prefer...]
    ppermute x2, waiting for transfers between devices: 6.24 us -> 0.06 us  [from_behind(): return lax.ppermute(block, axis, route)]
    ppermute x0 -> x2, starting transfers between devices: none -> 6.05 us  [swap(): return lax.ppermute(values_in, 'ctx', [(i, i ^ 4) for i in range(32)])]
  transfers between devices with their start and end apart: 6 -> 4, of which waited for: 5 -> 1; matrix products, arithmetic and copies ran while one was open for 7% -> 10% of each run, Pallas kernels for 6% -> 46%
where the time goes in v2:
time: 158 us; the launch traced here: 155 us
  Pallas kernels  119 us (75%)
  other arithmetic  12.4 us (8%)
  starting transfers between devices  11.2 us (7%)
  local copies, waits for them, and re-layouts  6.6 us (4%)
  matrix products  5.26 us (3%)
    pallas_call x7, Pallas kernels, call(): pl.pallas_call(kern, out_shape=jax.ShapeDtypeStruct(out, BF), in_specs=[p...  103 us
    pallas_call x1, Pallas kernels, long_backward(): pl.pallas_call(kb, out_shape=(jax.ShapeDtypeStruct((NB, OWN, T), BF), jax...  10.8 us
    ppermute x2, starting transfers between devices, swap(): return lax.ppermute(values_in, 'ctx', [(i, i ^ 4) for i in range(32)])  6.05 us
    convert_element_type x1, other arithmetic, short_forward(): return summed.astype(jnp.bfloat16)  5.73 us
    convert_element_type x1, other arithmetic, short_backward(): return summed.astype(jnp.bfloat16)  5.49 us
    ppermute x2, starting transfers between devices, from_behind(): return lax.ppermute(block, axis, route)  5.2 us
    pallas_call x1, Pallas kernels, long_forward(): pl.pallas_call(kf, out_shape=jax.ShapeDtypeStruct((NB, OWN, T), BF), scra...  4.86 us
    dot_general x1, matrix products, local(): jnp.einsum('sco,bsot->bct', weights, cot.reshape(2, 16, 128, 128), prefer...  3.47 us
  transfers between devices with their start and end apart: 4, of which 1 were waited for; matrix products, arithmetic and copies ran while one was open for 10% of the time, Pallas kernels for 46%

profile of v2, /device:TPU:0, one launch (start us, length us, event | category | flops | bytes accessed | tf_op | source)
XLA Modules:
  0.0 155.2 jit_solution(5460912941888414027)
XLA Ops:
  0.6 0.0 copy-start
  0.6 0.0 copy-start.3
  0.7 1.5 slice.84
  2.1 0.3 copy.61
  2.4 3.9 %collective-permute-start = (bf16[3,1024,6]{1,2,0:T(8,128)(2,1)S(1)}, bf16[3,1024,6]{1,2,0:T(8,128)(2,1)S(1)}, u32[]{:S(2)}, u32[]{:S(2)}) collective-permute-start(bf16[3,1024,6]{1,2,0:T(8,128)(2,1)S(1)} %copy.61), channel_id=1, source_target_pairs={{0,4},{4,8},{8,12},{12,16},{16,20},{20,24},{24,28},{28,32},{32,36}... | collective-permute-start | bytes 110600 | tf_op jit(solution)/shard_map/ppermute | solution.py:15
  6.4 0.0 copy-done.3
  6.4 0.0 copy-start.4
  6.4 28.9 %relay_kernel.1 = bf16[16,1024,128]{2,1,0:T(8,128)(2,1)S(1)} custom-call(bf16[1024,128]{1,0:T(8,128)(2,1)S(1)} %copy-done.3), custom_call_target="tpu_custom_call" | custom-call | tf_op jit(solution)/shard_map/relay_kernel/pallas_call | solution.py:325
  35.3 1.9 %copy-done.1 = bf16[16,1024,128]{2,1,0:T(8,128)(2,1)} copy-done((bf16[16,1024,128]{2,1,0:T(8,128)(2,1)}, bf16[16,1024,128]{2,1,0:T(8,128)(2,1)S(1)}, u32[]{:S(2)}) %copy-start.1) | copy-done | bytes 4194328
  37.3 0.0 copy-done.4
  37.3 16.0 %ygroup_kernel.1 = bf16[2,2048,128]{2,1,0:T(8,128)(2,1)S(1)} custom-call(bf16[1024,128]{1,0:T(8,128)(2,1)S(1)} %copy-done.4), custom_call_target="tpu_custom_call" | custom-call | tf_op jit(solution)/shard_map/ygroup_kernel/pallas_call | solution.py:325
  53.3 0.0 copy-start.7
  53.3 3.5 %fusion.2 = f32[2,128,1024]{1,2,0:T(8,128)S(1)} fusion(bf16[2,16,128,128]{3,2,1,0:T(8,128)(2,1)S(1)} %bitcast.81, bf16[16,1024,128]{2,1,0:T(8,128)(2,1)} %copy-done.1), kind=kOutput, calls=%fused_computation.16 | convolution fusion | flops 1073741824 | bytes 6291456 | tf_op jit(solution)/shard_map/sco,bsot->bct/dot_general | solution.py:359
  56.8 0.0 copy-start.6
  56.9 1.4 collective-permute-start.2
  58.3 0.1 fusion.23
  58.4 0.1 dynamic-slice_bitcast_fusion
  58.5 0.1 copy.36.skip
  58.6 0.0 collective-permute-done
  58.6 0.4 copy.35
  59.0 0.0 copy-start.5
  59.0 5.7 %add_convert_fusion.1 = bf16[3,1024,128]{2,1,0:T(8,128)(2,1)S(1)} fusion(bf16[3,1024,128]{2,1,0:T(8,128)(2,1)S(1)} %copy-done.6, bf16[3,1024,6]{2,1,0:T(8,128)(2,1)S(1)} %copy.35, f32[3,1024]{1,0:T(4,128)S(1)} %get-tuple-element.22, f32[3,1024]{1,0:T(4,128)S(1)} %get-tuple-element.23, f32[3,1024]{1,0:T(4,128)S(1)} %get-tuple-element.24, ...), kind=kLoop, calls=%fused_computation.14 | loop fusion | flops 15335424 | bytes 1695744 | tf_op jit(solution)/shard_map/convert_element_type | solution.py:32
  64.8 0.1 fusion.10
  64.8 11.2 %a2a_kernel.4.own = bf16[32,32,128]{2,1,0:T(8,128)(2,1)S(1)} custom-call(bf16[32,32,128]{2,1,0:T(8,128)(2,1)S(1)} %bitcast.84), custom_call_target="tpu_custom_call" | custom-call | tf_op jit(solution)/shard_map/a2a_kernel/pallas_call | solution.py:325
  76.0 4.9 %long_forward.1.v_ref = bf16[32,32,128]{2,1,0:T(8,128)(2,1)S(1)} custom-call(bf16[32,32,128]{2,1,0:T(8,128)(2,1)S(1)} %a2a_kernel.4.own, f32[2,4096]{1,0:T(2,128)S(1)} %bitcast.85, f32[32,1]{1,0:T(8,128)S(1)} %copy.36.skip), custom_call_target="tpu_custom_call" | custom-call | tf_op jit(solution)/shard_map/long_forward/pallas_call | solution.py:150
  80.9 10.4 %a2a_kernel.5 = bf16[32,32,128]{2,1,0:T(8,128)(2,1)S(1)} custom-call(bf16[32,32,128]{2,1,0:T(8,128)(2,1)S(1)} %long_forward.1.v_ref), custom_call_target="tpu_custom_call" | custom-call | tf_op jit(solution)/shard_map/a2a_kernel/pallas_call | solution.py:325
  91.3 0.0 collective-permute-done.2
  91.3 0.1 fusion.20
  91.5 0.2 fusion.13
  91.6 10.5 %a2a_kernel.6.down = bf16[32,32,128]{2,1,0:T(8,128)(2,1)S(1)} custom-call(bf16[32,32,128]{2,1,0:T(8,128)(2,1)S(1)} %bitcast.82), custom_call_target="tpu_custom_call" | custom-call | tf_op jit(solution)/shard_map/a2a_kernel/pallas_call | solution.py:325
  102.1 10.8 %long_backward.1 = (bf16[32,32,128]{2,1,0:T(8,128)(2,1)S(1)}, f32[2,4096]{1,0:T(2,128)}) custom-call(bf16[32,32,128]{2,1,0:T(8,128)(2,1)S(1)} %a2a_kernel.4.own, bf16[32,32,128]{2,1,0:T(8,128)(2,1)S(1)} %a2a_kernel.6.down, f32[2,4096]{1,0:T(2,128)S(1)} %bitcast.86, f32[32,1]{1,0:T(8,128)S(1)} %copy.36.skip), custom_call_target="tpu_custom_call" | custom-call | tf_op jit(solution)/shard_map/long_backward/pallas_call | solution.py:154
  113.0 10.2 %a2a_kernel.7 = bf16[32,32,128]{2,1,0:T(8,128)(2,1)S(1)} custom-call(bf16[32,32,128]{2,1,0:T(8,128)(2,1)S(1)} %get-tuple-element.5.v_ref), custom_call_target="tpu_custom_call" | custom-call | tf_op jit(solution)/shard_map/a2a_kernel/pallas_call | solution.py:325
  123.2 0.1 fusion.14
  123.3 0.1 pad_maximum_fusion.2
  123.4 0.3 copy.44
  123.7 1.3 collective-permute-start.3
  125.0 4.6 %collective-permute-start.1 = (bf16[1024,128]{1,0:T(8,128)(2,1)S(1)}, bf16[1024,128]{1,0:T(8,128)(2,1)S(1)}, u32[]{:S(2)}, u32[]{:S(2)}) collective-permute-start(bf16[1024,128]{1,0:T(8,128)(2,1)S(1)} %get-tuple-element.12), channel_id=1, source_target_pairs={{0,16},{4,20},{8,24},{12,28},{16,0},{20,4},{24,8},{28,12},{32,48},... | collective-permute-start | bytes 786440 | tf_op jit(solution)/shard_map/ppermute | solution.py:342
  129.6 0.1 collective-permute-done.3
  129.7 0.4 copy.45
  130.1 0.3 pad_maximum_fusion
  130.4 5.5 %add_convert_fusion = bf16[3,1024,128]{2,1,0:T(8,128)(2,1)} fusion(bf16[3,1024,134]{2,1,0:T(8,128)(2,1)S(1)} %pad_maximum_fusion, f32[3,1024]{1,0:T(4,128)S(1)} %get-tuple-element.22, f32[3,1024]{1,0:T(4,128)S(1)} %get-tuple-element.23, f32[3,1024]{1,0:T(4,128)S(1)} %get-tuple-element.24, f32[3,1024]{1,0:T(4,128)S(1)} %get-tuple-element.25, ...), kind=kLoop, calls=%fused_computation.13 | loop fusion | flops 9043968 | bytes 6377472 | tf_op jit(solution)/shard_map/convert_element_type | solution.py:44
  135.9 0.0 collective-permute-done.1
  136.0 0.0 copy-done.2
  136.0 1.8 %convolution_convert_fusion = bf16[2,128,4,4,128]{1,4,3,2,0:T(8,128)(2,1)S(1)} fusion(bf16[4,4,1024,128,1]{3,2,1,0,4:T(8,128)(2,1)S(1)} %bitcast.80, bf16[1,1024,128]{2,1,0:T(8,128)(2,1)S(1)} %get-tuple-element.14, bf16[1,1024,128]{2,1,0:T(8,128)(2,1)S(1)} %get-tuple-element.13), kind=kOutput, calls=%fused_computation.15 | convolution fusion | flops 1075314688 | bytes 5767168 | tf_op jit(solution)/shard_map/bct,pzco->bptzo/dot_general | solution.py:374
  137.8 0.5 copy.51.v_ref
  138.3 15.8 %spread_kernel.1 = bf16[2,4,128,512]{3,2,1,0:T(8,128)(2,1)S(1)} custom-call(bf16[2,4,128,512]{3,2,1,0:T(8,128)(2,1)S(1)} %copy.51.v_ref), custom_call_target="tpu_custom_call" | custom-call | tf_op jit(solution)/shard_map/spread_kernel/pallas_call | solution.py:325
  154.1 0.3 reduce_sum.12
  154.4 0.8 copy.39
  (12 shorter events, 0.1 us)
Async XLA Ops:
  0.6 57.8 %copy-start = (f32[1024]{0:T(1024)S(1)}, f32[1024]{0:T(1024)}, u32[]{:S(2)}) copy-start(f32[1024]{0:T(1024)} %param.9) | copy-start | bytes 12292
  0.6 5.7 %copy-start.3 = (bf16[1024,128]{1,0:T(8,128)(2,1)S(1)}, bf16[1024,128]{1,0:T(8,128)(2,1)}, u32[]{:S(2)}) copy-start(bf16[1024,128]{1,0:T(8,128)(2,1)} %w_ref.1) | copy-start | bytes 786436
  2.4 56.2 %collective-permute-start = (bf16[3,1024,6]{1,2,0:T(8,128)(2,1)S(1)}, bf16[3,1024,6]{1,2,0:T(8,128)(2,1)S(1)}, u32[]{:S(2)}, u32[]{:S(2)}) collective-permute-start(bf16[3,1024,6]{1,2,0:T(8,128)(2,1)S(1)} %copy.61), channel_id=1, source_target_pairs={{0,4},{4,8},{8,12},{12,16},{16,20},{20,24},{24,28},{28,32},{32,36}... | collective-permute-start | bytes 110600 | tf_op jit(solution)/shard_map/ppermute | solution.py:15
  6.4 30.9 %copy-start.4 = (bf16[1024,128]{1,0:T(8,128)(2,1)S(1)}, bf16[1024,128]{1,0:T(8,128)(2,1)}, u32[]{:S(2)}) copy-start(bf16[1024,128]{1,0:T(8,128)(2,1)} %v_ref.1) | copy-start | bytes 786436
  35.3 2.0 %copy-start.1 = (bf16[16,1024,128]{2,1,0:T(8,128)(2,1)}, bf16[16,1024,128]{2,1,0:T(8,128)(2,1)S(1)}, u32[]{:S(2)}) copy-start(bf16[16,1024,128]{2,1,0:T(8,128)(2,1)S(1)} %relay_kernel.1) | copy-start | bytes 12582916
  53.3 5.0 %copy-start.7 = (f32[7,3,1024]{2,0,1:T(8,128)S(1)}, f32[7,3,1024]{2,0,1:T(8,128)}, u32[]{:S(2)}) copy-start(f32[7,3,1024]{2,0,1:T(8,128)} %param.7) | copy-start | bytes 258052
  56.8 2.2 %copy-start.6 = (bf16[3,1024,128]{2,1,0:T(8,128)(2,1)S(1)}, bf16[3,1024,128]{2,1,0:T(8,128)(2,1)}, u32[]{:S(2)}) copy-start(bf16[3,1024,128]{2,1,0:T(8,128)(2,1)} %param.6) | copy-start | bytes 2359300
  56.9 34.5 %collective-permute-start.2 = (bf16[1024,128]{1,0:T(8,128)(2,1)S(1)}, bf16[1024,128]{1,0:T(8,128)(2,1)S(1)}, u32[]{:S(2)}, u32[]{:S(2)}) collective-permute-start(bf16[1024,128]{1,0:T(8,128)(2,1)S(1)} %fusion.19), channel_id=1, source_target_pairs={{0,16},{4,20},{8,24},{12,28},{16,0},{20,4},{24,8},{28,12},{32,48},... | collective-permute-start | bytes 786440 | tf_op jit(solution)/shard_map/ppermute | solution.py:342
  59.0 17.0 %copy-start.5 = (f32[1,2,4096]{2,1,0:T(2,128)S(1)}, f32[1,2,4096]{2,1,0:T(2,128)}, u32[]{:S(2)}) copy-start(f32[1,2,4096]{2,1,0:T(2,128)} %param.8) | copy-start | bytes 98308
  123.7 6.0 %collective-permute-start.3 = (bf16[3,1024,6]{1,2,0:T(8,128)(2,1)S(1)}, bf16[3,1024,6]{1,2,0:T(8,128)(2,1)S(1)}, u32[]{:S(2)}, u32[]{:S(2)}) collective-permute-start(bf16[3,1024,6]{1,2,0:T(8,128)(2,1)S(1)} %copy.44), channel_id=1, source_target_pairs={{4,0},{8,4},{12,8},{16,12},{20,16},{24,20},{28,24},{32,28},{36,32}... | collective-permute-start | bytes 110600 | tf_op jit(solution)/shard_map/ppermute | solution.py:15
  125.0 10.9 %collective-permute-start.1 = (bf16[1024,128]{1,0:T(8,128)(2,1)S(1)}, bf16[1024,128]{1,0:T(8,128)(2,1)S(1)}, u32[]{:S(2)}, u32[]{:S(2)}) collective-permute-start(bf16[1024,128]{1,0:T(8,128)(2,1)S(1)} %get-tuple-element.12), channel_id=1, source_target_pairs={{0,16},{4,20},{8,24},{12,28},{16,0},{20,4},{24,8},{28,12},{32,48},... | collective-permute-start | bytes 786440 | tf_op jit(solution)/shard_map/ppermute | solution.py:342
  130.4 5.5 %copy-start.2 = (bf16[16,1024,128]{2,1,0:T(8,128)(2,1)S(1)}, bf16[16,1024,128]{2,1,0:T(8,128)(2,1)}, u32[]{:S(2)}) copy-start(bf16[16,1024,128]{2,1,0:T(8,128)(2,1)} %copy-done.1) | copy-start | bytes 12582916

commit v3 on v1

v3 whole, which is shorter than its diff:
```python
import math

import jax
import jax.numpy as jnp
from jax import lax
from jax.experimental import pallas as pl
from jax.experimental.pallas import tpu as pltpu
from jax.sharding import PartitionSpec as P

BF, F32 = jnp.bfloat16, jnp.float32
MESH = pl.DeviceIdType.MESH
NB = 32
OWN = 32
G = 2
T = 128
C = 1024
TAPS = 7
SCALE = 1.0 / math.sqrt(16 * 4096)


def dot(a, b, ca, cb):
    return lax.dot_general(a, b, (((ca,), (cb,)), ((), ())), preferred_element_type=F32)


def at(value, multiple):
    return pl.multiple_of(value, multiple)


def build_toeplitz(h_ref, hpad, M):
    for g in range(G):
        hpad[g:g + 1, 0:128] = jnp.zeros((1, 128), F32)
        hpad[g:g + 1, 128:] = h_ref[g:g + 1, :]
        M[g, 128:256, 0:128] = jnp.zeros((128, 128), BF)
    def step(e, c):
        for g in range(G):
            seg = hpad[g:g + 1, pl.ds(pl.multiple_of(e * 128, 128), 256)]
            tile = pltpu.roll(jnp.broadcast_to(seg, (128, 256)), 0, 1, stride=1, stride_axis=0)[:, 128:].astype(BF)
            M[g, 0:128, pl.ds(pl.multiple_of(e * 128, 128), 128)] = tile
            M[g, 128:256, pl.ds(pl.multiple_of(e * 128 + 128, 128), 128)] = tile
        return c
    lax.fori_loop(0, NB, step, 0)


def load_pairs(own, X, row0):
    for g in range(G):
        for h in range(2):
            v = own[...].reshape(NB // 2, 2, OWN, T)[:, h, 16 * g:16 * g + 16, :]
            X[g, row0:row0 + 256, T * h:T * h + T] = v.reshape(256, T)


def store_pairs(y, out, g):
    for j in range(NB // 2):
        for h in range(2):
            out[2 * j + h, 16 * g:16 * g + 16, :] = y[16 * j:16 * j + 16, T * h:T * h + T].astype(out.dtype)


def conv_forward(X, M, skip_rows, out):
    for g in range(G):
        acc = jnp.zeros((256, 256), F32)
        for d in range(16):
            acc = acc + dot(X[g, 256 - 16 * d:512 - 16 * d, :], M[g, :, 256 * d:256 * d + 256], 1, 0)
        y = acc + skip_rows(g) * X[g, 256:512, :].astype(F32)
        store_pairs(y, out, g)


def conv_backward(D, M, skip_rows, out):
    for g in range(G):
        acc = jnp.zeros((256, 256), F32)
        for d in range(16):
            acc = acc + dot(D[g, 16 * d:16 * d + 256, :], M[g, :, 256 * d:256 * d + 256], 1, 1)
        y = acc + skip_rows(g) * D[g, 0:256, :].astype(F32)
        store_pairs(y, out, g)


def filter_gradient(X, D, XR, carry, gacc, out, scaling):
    rows = lax.broadcasted_iota(jnp.int32, (256, 256), 0)
    cols = lax.broadcasted_iota(jnp.int32, (256, 256), 1)
    flip = jnp.where(rows + cols == 255, 1.0, 0.0).astype(BF)
    for g in range(G):
        XR[g] = dot(flip, X[g, 256:512, :], 1, 1).astype(BF)
    gacc[...] = jnp.zeros(gacc.shape, F32)
    carry[...] = jnp.zeros(carry.shape, F32)
    def shear(tile):
        wide = jnp.concatenate([tile, jnp.zeros((128, 128), F32)], axis=1)
        return jnp.sum(pltpu.roll(wide, 1, 1, stride=1, stride_axis=0), axis=0, keepdims=True)
    def step(d, c):
        for g in range(G):
            p = dot(XR[g], D[g, pl.ds(pl.multiple_of(16 * d, 16), 256), :], 1, 0)
            at = pl.multiple_of(256 * d, 128)
            gacc[g:g + 1, pl.ds(at, 256)] += shear(p[0:128, 0:128] + carry[g])
            at = pl.multiple_of(256 * d + 128, 128)
            gacc[g:g + 1, pl.ds(at, 256)] += shear(p[0:128, 128:] + p[128:, 0:128])
            carry[g] = p[128:, 128:]
        return c
    lax.fori_loop(0, 16, step, 0)
    for g in range(G):
        last = shear(carry[g])
        gacc[g:g + 1, 4096:4352] += last
        out[g:g + 1, :] = gacc[g:g + 1, 256:4352] * scaling

class Place:
    def __init__(self):
        self.ctx = lax.axis_index("ctx")
        self.tp = lax.axis_index("tp")
        self.x = self.ctx // 8
        self.lo = (self.ctx // 4) % 2
        self.z = self.ctx % 4
        self.partner = self.ctx + 4 - 8 * self.lo

    def plane(self, x, z):
        return x * 8 + self.lo * 4 + z


def barrier_signals(me):
    sem = pltpu.get_barrier_semaphore()

    def one(k, c):
        pl.semaphore_signal(sem, inc=1, device_id=((me.ctx + k) % NB, me.tp), device_id_type=MESH)
        return c

    lax.fori_loop(1, NB, one, 0)
    for k in (1, 2, 3):
        for ctx in (me.ctx, me.partner):
            pl.semaphore_signal(sem, inc=1, device_id=(ctx, (me.tp + k) % 4), device_id_type=MESH)
    return sem


class Relay:
    def __init__(self, me, w, wg, ssem, rsem):
        self.me, self.w, self.wg, self.ssem, self.rsem = me, w, wg, ssem, rsem
        self.sends = []
        self.first = [None, None]
        self.fwd = [[None, None], [None, None]]
        self.second = [{}, {}]
        self.last = [{}, {}]

    def slot(self, h, f, s):
        me = self.me
        if h == 0:
            return ((me.x + s) % 4) * 4 + (me.z + f) % 4
        return ((me.x + f) % 4) * 4 + (me.z + s) % 4

    def dev(self, h, f, s):
        me = self.me
        if h == 0:
            return me.plane((me.x + s) % 4, (me.z + f) % 4)
        return me.plane((me.x + f) % 4, (me.z + s) % 4)

    def send(self, src, dst, dev):
        n = len(self.sends)
        c = pltpu.make_async_remote_copy(
            src_ref=src, dst_ref=dst, send_sem=self.ssem.at[n], recv_sem=self.rsem.at[n],
            device_id=(dev, self.me.tp), device_id_type=MESH)
        c.start()
        self.sends.append(c)
        return c

    def part(self, b, r, n):
        return self.wg.at[b, pl.ds(r, n), :]

    def own(self, h):
        return self.w.at[pl.ds(512 * h, 512), :]

    def pair(self, h, f):
        b = self.slot(h, f, 0)
        dst = self.part(b, 512 * h, 512)
        src = self.own(h) if f == 0 else dst
        self.second[h][f] = [self.send(src, dst, self.dev(h, 0, 1)), self.send(src, dst, self.dev(h, 0, -1))]

    def begin(self):
        for h in (0, 1):
            dst = self.part(self.slot(h, 0, 0), 512 * h, 512)
            self.first[h] = [self.send(self.own(h), dst, self.dev(h, 1, 0)), self.send(self.own(h), dst, self.dev(h, -1, 0))]
        for h in (0, 1):
            self.pair(h, 0)

    def neighbours(self):
        for i, f in ((0, -1), (1, 1)):
            for h in (0, 1):
                self.first[h][i].wait_recv()
                part = self.part(self.slot(h, f, 0), 512 * h + 256 * i, 256)
                self.fwd[h][i] = self.send(part, part, self.dev(h, -f, 0))
                self.pair(h, f)

    def opposite(self):
        for h in (0, 1):
            for i in (0, 1):
                self.fwd[h][i].wait_recv()
            self.pair(h, 2)

    def forward(self, h, f):
        cs = []
        for i, s in ((0, -1), (1, 1)):
            self.second[h][f][i].wait_recv()
            part = self.part(self.slot(h, f, s), 512 * h + 256 * i, 256)
            cs.append(self.send(part, part, self.dev(h, 0, -s)))
        self.last[h][f] = cs

    def finish(self, h, f):
        for c in self.last[h][f]:
            c.wait_recv()


class Exchange:
    def __init__(self, me, src, dst, ssem, rsem):
        self.me, self.src, self.dst, self.ssem, self.rsem = me, src, dst, ssem, rsem

    def send(self, to):
        pltpu.make_async_remote_copy(
            src_ref=self.src.at[to], dst_ref=self.dst.at[self.me.ctx], send_sem=self.ssem, recv_sem=self.rsem,
            device_id=(to, self.me.tp), device_id_type=MESH).start()

    def start(self):
        def go(k, c):
            self.send((self.me.ctx + k) % NB)
            return c

        lax.fori_loop(1, NB, go, 0)
        self.dst[self.me.ctx] = self.src[self.me.ctx]

    def all(self):
        return pltpu.make_async_remote_copy(
            src_ref=self.src.at[pl.ds(0, NB - 1)], dst_ref=self.dst.at[pl.ds(0, NB - 1)], send_sem=self.ssem,
            recv_sem=self.rsem, device_id=(self.me.partner, self.me.tp), device_id_type=MESH)


def group_copies(me, pick, dst, ssem, rsem):
    cs = []
    for same in (1, 0):
        for k in range(same, 4):
            lo = me.lo if same else 1 - me.lo
            tp = (me.tp + k) % 4
            cs.append(pltpu.make_async_remote_copy(
                src_ref=pick(lo, tp), dst_ref=dst, send_sem=ssem.at[len(cs)], recv_sem=rsem.at[len(cs)],
                device_id=(me.ctx if same else me.partner, tp), device_id_type=MESH))
    return cs


def lanes(shape):
    return lax.broadcasted_iota(jnp.int32, shape, len(shape) - 1)


def picker(first):
    rows = lax.broadcasted_iota(jnp.int32, (16, T), 0)
    return jnp.where(lanes((16, T)) == rows + first, 1.0, 0.0).astype(BF)


def taps_to_rows(cw, cwt):
    for b in range(C // T):
        rows = [cw[j, s:s + 1, T * b:T * b + T] for j in range(TAPS) for s in range(3)]
        block = jnp.concatenate(rows + [jnp.zeros((T - len(rows), T), F32)], axis=0)
        cwt[T * b:T * b + T, :] = block.T


def short_rows(s, rows, x, rim, cwt, backward):
    lane = lanes((T, T))
    total = cwt[rows, s:s + 1] * x
    for j in range(1, TAPS):
        if backward:
            shifted = pltpu.roll(jnp.where(lane < j, rim, x), T - j, 1)
        else:
            shifted = pltpu.roll(jnp.where(lane >= T - j, rim, x), j, 1)
        total = total + cwt[rows, 3 * j + s:3 * j + s + 1] * shifted
    return total


def kernel(proj, cw, filt, skip, w, cot, block_out, proj_grad, filter_grad,
           wg, cotg, rim_s, rim_r, short, mix_s, mix_r, long_s, long_r, gated, acc, part_s, part_r, dgated,
           dlong_s, dlong_r, dmix_s, dmix_r, dshort, share_s, share_r, cwt, hpad, M, X, D, XR, carry, gacc,
           relay_ss, relay_rs, x_ss, x_rs, cot_ss, cot_rs, share_ss, share_rs, rim_ss, rim_rs, part_ss, part_rs,
           gated_ss, gated_rs):
    me = Place()
    sem = barrier_signals(me)
    ahead, behind = (me.ctx + 1) % NB, (me.ctx + NB - 1) % NB

    def rim_copy(n, streams, to):
        return pltpu.make_async_remote_copy(
            src_ref=rim_s.at[streams], dst_ref=rim_r.at[streams], send_sem=rim_ss.at[n], recv_sem=rim_rs.at[n],
            device_id=(to, me.tp), device_id_type=MESH)

    last16, first16 = picker(T - 16), picker(0)
    for s in range(3):
        rim_s[s] = dot(last16, proj[s], 1, 1).astype(BF)
    pl.semaphore_wait(sem, NB - 1 + 6)

    relay = Relay(me, w, wg, relay_ss, relay_rs)
    rim0 = rim_copy(0, pl.ds(0, 3), ahead)
    rim0.start()
    relay.begin()
    cots = group_copies(me, lambda lo, tp: cot.at[pl.ds(at(512 * lo, 512), 512), :],
                        cotg.at[me.lo, pl.ds(at(512 * me.tp, 512), 512), :], cot_ss, cot_rs)
    for c in cots:
        c.start()

    wg[me.x * 4 + me.z] = w[...]
    cotg[me.lo, pl.ds(at(512 * me.tp, 512), 512), :] = cot[pl.ds(at(512 * me.lo, 512), 512), :]
    taps_to_rows(cw, cwt)
    build_toeplitz(filt, hpad, M)
    X[:, 0:256, :] = jnp.zeros((G, 256, 256), BF)
    D[:, 256:512, :] = jnp.zeros((G, 256, 256), BF)
    own_rows = lax.broadcasted_iota(jnp.int32, (OWN, C), 0) + me.ctx * OWN
    skip_own = jnp.sum(jnp.where(lanes((OWN, C)) == own_rows, skip[...], 0.0), axis=1, keepdims=True)

    def skip_rows(g):
        return jnp.broadcast_to(skip_own[None, 16 * g:16 * g + 16, :], (16, 16, 256)).reshape(256, 256)

    rim0.wait_recv()

    def short_step(r, c):
        rows = pl.ds(at(T * r, T), T)
        outs = []
        for s in range(3):
            rim = dot(rim_r[s, :, rows], last16, 0, 0)
            rim = jnp.where(me.ctx == 0, 0.0, rim)
            out = short_rows(s, rows, proj[s, rows, :].astype(F32), rim, cwt, False).astype(BF)
            short[s, rows, :] = out
            outs.append(out)
        mix = (outs[1].astype(F32) * outs[2].astype(F32)).astype(BF)
        mix_s[pl.ds(4 * r, 4)] = mix.reshape(4, OWN, T)
        return c

    lax.fori_loop(0, C // T, short_step, 0)
    relay.neighbours()
    mix_x = Exchange(me, mix_s, mix_r, x_ss.at[0], x_rs.at[0])
    mix_x.start()
    for h in (0, 1):
        relay.forward(h, 0)
    relay.opposite()

    mix_x.all().wait_recv()
    load_pairs(mix_r, X, 256)
    conv_forward(X, M, skip_rows, long_s)
    long_x = Exchange(me, long_s, long_r, x_ss.at[1], x_rs.at[1])
    long_x.start()
    for h in (0, 1):
        relay.forward(h, -1)
    for h in (0, 1):
        relay.forward(h, 1)
    for c in cots:
        c.wait_recv()

    def slots(h, f):
        me_f = (me.z + f) % 4 if h == 0 else (me.x + f) % 4
        return [(k * 4 + me_f) if h == 0 else (me_f * 4 + k) for k in range(4)]

    def columns(h, f):
        found = slots(h, f)
        return jnp.concatenate([
            jnp.concatenate([cotg[b, pl.ds(at(s * T, T), T), :] for s in found], axis=0) for b in (0, 1)], axis=1)

    def partial(h, f, r):
        left = jnp.concatenate([wg[s, r:r + 256, :] for s in slots(h, f)], axis=1)
        return left

    def contract(h, f, first):
        right = columns(h, f)
        for r in (512 * h, 512 * h + 256):
            value = dot(partial(h, f, r), right, 1, 0)
            if first:
                acc[r:r + 256, :] = value
            else:
                acc[r:r + 256, :] += value

    long_x.all().wait_recv()

    def gated_step(r, c):
        rows = pl.ds(at(T * r, T), T)
        value = short[0, rows, :].astype(F32) * long_r[pl.ds(4 * r, 4)].reshape(T, T).astype(F32)
        gated[me.lo, :, rows] = value.T.astype(BF)
        return c

    lax.fori_loop(0, C // T, gated_step, 0)
    gated_c = pltpu.make_async_remote_copy(
        src_ref=gated.at[me.lo], dst_ref=gated.at[me.lo], send_sem=gated_ss, recv_sem=gated_rs,
        device_id=(me.partner, me.tp), device_id_type=MESH)
    gated_c.start()
    for h in (0, 1):
        relay.forward(h, 2)
    for n, f in enumerate((0, -1, 1)):
        for h in (0, 1):
            relay.finish(h, f)
            contract(h, f, n == 0)

    parts = []
    for h in (0, 1):
        relay.finish(h, 2)
        right = columns(h, 2)
        for r in (512 * h, 512 * h + 256):
            value = acc[r:r + 256, :] + dot(partial(h, 2, r), right, 1, 0)
            theirs = jnp.where(me.lo == 0, value[:, T:], value[:, :T])
            part_s[r:r + 256, :] = theirs.astype(BF)
            n = len(parts)
            c = pltpu.make_async_remote_copy(
                src_ref=part_s.at[pl.ds(r, 256), :], dst_ref=part_r.at[pl.ds(r, 256), :], send_sem=part_ss.at[n],
                recv_sem=part_rs.at[n], device_id=(me.partner, me.tp), device_id_type=MESH)
            c.start()
            parts.append(c)
            acc[r:r + 256, 0:T] = jnp.where(me.lo == 0, value[:, :T], value[:, T:])

    dlong_x = Exchange(me, dlong_s, dlong_r, x_ss.at[2], x_rs.at[2])
    for n in range(4):
        parts[n].wait_recv()
        r = 256 * n
        value = (acc[r:r + 256, 0:T] + part_r[r:r + 256, :].astype(F32)).astype(BF)
        dgated[r:r + 256, :] = value
        value = (value.astype(F32) * short[0, r:r + 256, :].astype(F32)).astype(BF)
        dlong_s[8 * n:8 * n + 8] = value.reshape(8, OWN, T)
    dlong_x.start()

    def dq_step(r, c):
        rows = pl.ds(at(T * r, T), T)
        value = dgated[rows, :].astype(F32) * long_r[pl.ds(4 * r, 4)].reshape(T, T).astype(F32)
        dshort[0, rows, :] = value.astype(BF)
        return c

    lax.fori_loop(0, C // T, dq_step, 0)
    rim_s[3] = dot(first16, dshort[0], 1, 1).astype(BF)
    rim1 = rim_copy(1, pl.ds(3, 1), behind)
    rim1.start()

    gated_c.wait_recv()
    left = gated[...].reshape(2 * T, C)
    for x in range(4):
        for p in (0, 1):
            right = jnp.concatenate([wg[4 * x + 2 * p], wg[4 * x + 2 * p + 1]], axis=1)
            value = dot(left, right, 1, 0).astype(BF)
            for b in (0, 1):
                share_s[b, x, :, 256 * p:256 * p + 256] = value[T * b:T * b + T, :]
    share_r[me.lo, me.tp] = share_s[me.lo, me.tp]

    def grad_step(s):
        def step(r, c):
            rows = pl.ds(at(T * r, T), T)
            rim = dot(rim_r[3 + s, :, rows], first16, 0, 0)
            rim = jnp.where(me.ctx == NB - 1, 0.0, rim)
            out = short_rows(s, rows, dshort[s, rows, :].astype(F32), rim, cwt, True)
            proj_grad[s, rows, :] = out.astype(BF)
            return c
        return step

    dlong_x.all().wait_recv()
    shares = group_copies(me, lambda lo, tp: share_s.at[lo, tp], share_r.at[me.lo, me.tp], share_ss, share_rs)
    for c in shares:
        c.start()
    load_pairs(dlong_r, D, 0)
    conv_backward(D, M, skip_rows, dmix_s)
    dmix_x = Exchange(me, dmix_s, dmix_r, x_ss.at[3], x_rs.at[3])
    dmix_x.start()
    filter_gradient(X, D, XR, carry, gacc, filter_grad, SCALE)
    rim1.wait_recv()
    lax.fori_loop(0, C // T, grad_step(0), 0)

    dmix_x.all().wait_recv()

    def dkv_step(r, c):
        rows = pl.ds(at(T * r, T), T)
        value = dmix_r[pl.ds(4 * r, 4)].reshape(T, T).astype(F32)
        for s in (1, 2):
            dshort[s, rows, :] = (value * short[3 - s, rows, :].astype(F32)).astype(BF)
        return c

    lax.fori_loop(0, C // T, dkv_step, 0)
    for s in (1, 2):
        rim_s[3 + s] = dot(first16, dshort[s], 1, 1).astype(BF)
    rim2 = rim_copy(2, pl.ds(4, 2), behind)
    rim2.start()
    for c in shares:
        c.wait_recv()
    for b in (0, 1):
        for k in range(4):
            cols = slice(T * k, T * k + T)
            value = share_r[b, 0, :, cols].astype(F32)
            for tp in (1, 2, 3):
                value = value + share_r[b, tp, :, cols].astype(F32)
            block_out[512 * b + T * k:512 * b + T * k + T, :] = value.T.astype(BF)
    rim2.wait_recv()
    for s in (1, 2):
        lax.fori_loop(0, C // T, grad_step(s), 0)
    for c in [rim0, rim1, rim2, gated_c] + relay.sends + cots + parts + shares:
        c.wait_send()
    for x in (mix_x, long_x, dlong_x, dmix_x):
        x.all().wait_send()


def local(projected, conv_weight, filters, skip_gain, out_weight, cotangent):
    dma = pltpu.SemaphoreType.DMA
    vmem = pltpu.VMEM
    blocks = vmem((NB, OWN, T), BF)
    rows = vmem((C, T), BF)
    scratch = dict(
        wg=vmem((16, C, T), BF), cotg=vmem((2, 2048, T), BF), rim_s=vmem((6, 16, C), BF), rim_r=vmem((6, 16, C), BF),
        short=vmem((3, C, T), BF), mix_s=blocks, mix_r=blocks, long_s=blocks, long_r=blocks, gated=vmem((2, T, C), BF),
        acc=vmem((C, 2 * T), F32), part_s=rows, part_r=rows, dgated=rows, dlong_s=blocks, dlong_r=blocks, dmix_s=blocks,
        dmix_r=blocks, dshort=vmem((3, C, T), BF), share_s=vmem((2, 4, T, 512), BF), share_r=vmem((2, 4, T, 512), BF),
        cwt=vmem((C, T), F32), hpad=vmem((G, 4096 + T), F32), M=vmem((G, 256, 4096 + T), BF), X=vmem((G, 512, 256), BF),
        D=vmem((G, 512, 256), BF), XR=vmem((G, 256, 256), BF), carry=vmem((G, T, T), F32), gacc=vmem((G, 4352), F32),
        relay_ss=dma((40,)), relay_rs=dma((40,)), x_ss=dma((4,)), x_rs=dma((4,)), cot_ss=dma((7,)), cot_rs=dma((7,)),
        share_ss=dma((7,)), share_rs=dma((7,)), rim_ss=dma((3,)), rim_rs=dma((3,)), part_ss=dma((4,)), part_rs=dma((4,)),
        gated_ss=dma, gated_rs=dma)
    whole = pl.BlockSpec(memory_space=pltpu.VMEM)
    block_out, proj_grad, filter_grad = pl.pallas_call(
        kernel,
        out_shape=(
            jax.ShapeDtypeStruct((C, T), BF),
            jax.ShapeDtypeStruct((3, C, T), BF),
            jax.ShapeDtypeStruct((G, 4096), F32),
        ),
        in_specs=[whole] * 6,
        out_specs=(whole,) * 3,
        scratch_shapes=list(scratch.values()),
        compiler_params=pltpu.CompilerParams(collective_id=1, has_side_effects=True, vmem_limit_bytes=48 << 20),
        name="hyena_block",
    )(projected, conv_weight, filters[0], skip_gain[None], out_weight, cotangent)
    return block_out, proj_grad, filter_grad[None]


def solution(mesh):
    return jax.shard_map(
        local,
        mesh=mesh,
        in_specs=(
            P(None, "tp", "ctx"),
            P(None, None, "tp"),
            P("tp", "ctx", None),
            P("tp"),
            P("tp", "ctx"),
            P("tp", "ctx"),
        ),
        out_specs=(P("tp", "ctx"), P(None, "tp", "ctx"), P("tp", "ctx", None)),
        check_vma=False,
    )
```

time: 278 us -> 92.7 us (0.33)
  waiting for transfers between devices: 168 us -> 0 us
  Pallas kernels: 15.7 us -> 85.5 us
  blocking collectives: 43.6 us -> 0 us
  starting transfers between devices: 14.9 us -> 0 us
  between operations: 14 us -> 0.68 us
  matrix products: 12.2 us -> 0 us
  other arithmetic: 3.34 us -> 0 us
    all_gather x2 -> x0, waiting for transfers between devices: 151 us -> none  [the longest x1 134 us: local(): weight_full = lax.all_gather(out_weight, 'ctx', axis=1, tiled=True)]
    pallas_call x2 -> x1, Pallas kernels: 15.7 us -> 85.5 us  [local(): pl.pallas_call(kernel, out_shape=(jax.ShapeDtypeStruct((C, T), BF), jax.S...]
    all_to_all x3 -> x0, blocking collectives: 43.6 us -> none  [the longest x2 26.9 us: to_tokens(): lax.all_to_all(values_in, 'ctx', split_axis=0, concat_axis=0, tiled=True)]
    dot_general x2 -> x0, matrix products: 12.2 us -> none  [the longest x1 6.51 us: local(): jnp.dot(weight_cols, lax.all_gather(cotangent, 'tp', axis=0, tiled=True),...]
    all_to_all x1 -> x0, starting transfers between devices: 9.6 us -> none  [to_owners(): lax.all_to_all(values_in.reshape(ctx_size, channels // ctx_size, tokens),...]
    all_to_all x1 -> x0, waiting for transfers between devices: 9.25 us -> none  [to_owners(): lax.all_to_all(values_in.reshape(ctx_size, channels // ctx_size, tokens),...]
    ppermute x2 -> x0, waiting for transfers between devices: 6.24 us -> none  [from_behind(): return lax.ppermute(block, axis, route)]
    ppermute x2 -> x0, starting transfers between devices: 5.2 us -> none  [from_behind(): return lax.ppermute(block, axis, route)]
  transfers between devices with their start and end apart: 6 -> 0, of which waited for: 5 -> 0; matrix products, arithmetic and copies ran while one was open for 7% -> 0% of each run, Pallas kernels for 6% -> 0%
where the time goes in v3:
time: 92.7 us; the launch traced here: 92.4 us
  Pallas kernels  85.5 us (92%)
  local copies, waits for them, and re-layouts  6.2 us (7%)
    pallas_call x1, Pallas kernels, local(): pl.pallas_call(kernel, out_shape=(jax.ShapeDtypeStruct((C, T), BF), jax.S...  85.5 us
    unnamed x14, local copies, waits for them, and re-layouts  6.2 us

profile of v3, /device:TPU:0, one launch (start us, length us, event | category | flops | bytes accessed | tf_op | source)
XLA Modules:
  0.0 92.4 jit_solution(12979273640233756503)
XLA Ops:
  0.6 0.0 copy-start.3
  0.6 0.0 copy-start.4
  0.7 1.0 %copy.9.cw = f32[7,3,1024]{2,1,0:T(4,128)S(1)} copy(f32[7,3,1024]{2,0,1:T(8,128)} %param.7) | data formatting | bytes 172032 | tf_op args[1]
  1.6 0.0 copy-done.3
  1.6 0.0 copy-done.4
  1.6 0.0 copy-start
  1.7 1.1 %copy-done = bf16[3,1024,128]{2,1,0:T(8,128)(2,1)S(1)} copy-done((bf16[3,1024,128]{2,1,0:T(8,128)(2,1)S(1)}, bf16[3,1024,128]{2,1,0:T(8,128)(2,1)}, u32[]{:S(2)}) %copy-start) | copy-done | bytes 786456
  2.8 0.0 copy-start.1
  2.8 0.9 %copy-done.1 = bf16[1024,128]{1,0:T(8,128)(2,1)S(1)} copy-done((bf16[1024,128]{1,0:T(8,128)(2,1)S(1)}, bf16[1024,128]{1,0:T(8,128)(2,1)}, u32[]{:S(2)}) %copy-start.1) | copy-done | bytes 262168
  3.7 0.0 copy-start.2
  3.7 0.9 %copy-done.2 = bf16[1024,128]{1,0:T(8,128)(2,1)S(1)} copy-done((bf16[1024,128]{1,0:T(8,128)(2,1)S(1)}, bf16[1024,128]{1,0:T(8,128)(2,1)}, u32[]{:S(2)}) %copy-start.2) | copy-done | bytes 262168
  4.7 85.5 %hyena_block.1 = (bf16[1024,128]{1,0:T(8,128)(2,1)S(1)}, bf16[3,1024,128]{2,1,0:T(8,128)(2,1)S(1)}, f32[2,4096]{1,0:T(2,128)S(1)}) custom-call(bf16[3,1024,128]{2,1,0:T(8,128)(2,1)S(1)} %copy-done, f32[7,3,1024]{2,1,0:T(4,128)S(1)} %copy.9.cw, f32[2,4096]{1,0:T(2,128)S(1)} %bitcast.3, f32[1,1024]{1,0:T(1,128)S(1)} %bitcast.5, ...), custom_call_target="tpu_custom_call" | custom-call | tf_op jit(solution)/shard_map/hyena_block/pallas_call | solution.py:501
  90.2 0.7 copy.13
  90.9 0.9 copy.14
  91.8 0.6 copy.15
Async XLA Ops:
  0.6 1.0 %copy-start.3 = (f32[1,2,4096]{2,1,0:T(2,128)S(1)}, f32[1,2,4096]{2,1,0:T(2,128)}, u32[]{:S(2)}) copy-start(f32[1,2,4096]{2,1,0:T(2,128)} %param.8) | copy-start | bytes 98308
  0.6 1.0 %copy-start.4 = (f32[1024]{0:T(1024)S(1)}, f32[1024]{0:T(1024)}, u32[]{:S(2)}) copy-start(f32[1024]{0:T(1024)} %param.9) | copy-start | bytes 12292
  1.6 1.1 %copy-start = (bf16[3,1024,128]{2,1,0:T(8,128)(2,1)S(1)}, bf16[3,1024,128]{2,1,0:T(8,128)(2,1)}, u32[]{:S(2)}) copy-start(bf16[3,1024,128]{2,1,0:T(8,128)(2,1)} %proj.1) | copy-start | bytes 2359300
  2.8 0.9 %copy-start.1 = (bf16[1024,128]{1,0:T(8,128)(2,1)S(1)}, bf16[1024,128]{1,0:T(8,128)(2,1)}, u32[]{:S(2)}) copy-start(bf16[1024,128]{1,0:T(8,128)(2,1)} %w.1) | copy-start | bytes 786436
  3.7 0.9 %copy-start.2 = (bf16[1024,128]{1,0:T(8,128)(2,1)S(1)}, bf16[1024,128]{1,0:T(8,128)(2,1)}, u32[]{:S(2)}) copy-start(bf16[1024,128]{1,0:T(8,128)(2,1)} %cot.1) | copy-start | bytes 786436

commit v4 on v3

v4 whole, which is shorter than its diff:
```python
import math

import jax
import jax.numpy as jnp
from jax import lax
from jax.experimental import pallas as pl
from jax.experimental.pallas import tpu as pltpu
from jax.sharding import PartitionSpec as P

BF, F32 = jnp.bfloat16, jnp.float32
MESH = pl.DeviceIdType.MESH
NB = 32
OWN = 32
G = 2
T = 128
C = 1024
TAPS = 7
SCALE = 1.0 / math.sqrt(16 * 4096)


def dot(a, b, ca, cb):
    return lax.dot_general(a, b, (((ca,), (cb,)), ((), ())), preferred_element_type=F32)


def at(value, multiple):
    return pl.multiple_of(value, multiple)


def build_toeplitz(h_ref, hpad, M):
    for g in range(G):
        hpad[g:g + 1, 0:128] = jnp.zeros((1, 128), F32)
        hpad[g:g + 1, 128:] = h_ref[g:g + 1, :]
        M[g, 128:256, 0:128] = jnp.zeros((128, 128), BF)
    def step(e, c):
        for g in range(G):
            seg = hpad[g:g + 1, pl.ds(pl.multiple_of(e * 128, 128), 256)]
            tile = pltpu.roll(jnp.broadcast_to(seg, (128, 256)), 0, 1, stride=1, stride_axis=0)[:, 128:].astype(BF)
            M[g, 0:128, pl.ds(pl.multiple_of(e * 128, 128), 128)] = tile
            M[g, 128:256, pl.ds(pl.multiple_of(e * 128 + 128, 128), 128)] = tile
        return c
    lax.fori_loop(0, NB, step, 0)


def load_pairs(own, X, row0):
    for g in range(G):
        for h in range(2):
            v = own[...].reshape(NB // 2, 2, OWN, T)[:, h, 16 * g:16 * g + 16, :]
            X[g, row0:row0 + 256, T * h:T * h + T] = v.reshape(256, T)


def store_pairs(y, out, g):
    for j in range(NB // 2):
        for h in range(2):
            out[2 * j + h, 16 * g:16 * g + 16, :] = y[16 * j:16 * j + 16, T * h:T * h + T].astype(out.dtype)


def conv_forward(X, M, skip_rows, out):
    for g in range(G):
        acc = jnp.zeros((256, 256), F32)
        for d in range(16):
            acc = acc + dot(X[g, 256 - 16 * d:512 - 16 * d, :], M[g, :, 256 * d:256 * d + 256], 1, 0)
        y = acc + skip_rows(g) * X[g, 256:512, :].astype(F32)
        store_pairs(y, out, g)


def conv_backward(D, M, skip_rows, out):
    for g in range(G):
        acc = jnp.zeros((256, 256), F32)
        for d in range(16):
            acc = acc + dot(D[g, 16 * d:16 * d + 256, :], M[g, :, 256 * d:256 * d + 256], 1, 1)
        y = acc + skip_rows(g) * D[g, 0:256, :].astype(F32)
        store_pairs(y, out, g)


def filter_gradient(X, D, XR, carry, gacc, out, scaling):
    rows = lax.broadcasted_iota(jnp.int32, (256, 256), 0)
    cols = lax.broadcasted_iota(jnp.int32, (256, 256), 1)
    flip = jnp.where(rows + cols == 255, 1.0, 0.0).astype(BF)
    for g in range(G):
        XR[g] = dot(flip, X[g, 256:512, :], 1, 1).astype(BF)
    gacc[...] = jnp.zeros(gacc.shape, F32)
    carry[...] = jnp.zeros(carry.shape, F32)
    def shear(tile):
        wide = jnp.concatenate([tile, jnp.zeros((128, 128), F32)], axis=1)
        return jnp.sum(pltpu.roll(wide, 1, 1, stride=1, stride_axis=0), axis=0, keepdims=True)
    def step(d, c):
        for g in range(G):
            p = dot(XR[g], D[g, pl.ds(pl.multiple_of(16 * d, 16), 256), :], 1, 0)
            at = pl.multiple_of(256 * d, 128)
            gacc[g:g + 1, pl.ds(at, 256)] += shear(p[0:128, 0:128] + carry[g])
            at = pl.multiple_of(256 * d + 128, 128)
            gacc[g:g + 1, pl.ds(at, 256)] += shear(p[0:128, 128:] + p[128:, 0:128])
            carry[g] = p[128:, 128:]
        return c
    lax.fori_loop(0, 16, step, 0)
    for g in range(G):
        last = shear(carry[g])
        gacc[g:g + 1, 4096:4352] += last
        out[g:g + 1, :] = gacc[g:g + 1, 256:4352] * scaling


class Place:
    def __init__(self):
        self.ctx = lax.axis_index("ctx")
        self.tp = lax.axis_index("tp")
        self.x = self.ctx // 8
        self.lo = (self.ctx // 4) % 2
        self.z = self.ctx % 4
        self.hi = self.tp // 2
        self.core = self.tp % 2
        self.partner = self.ctx + 4 - 8 * self.lo
        self.sibling = self.tp + 1 - 2 * self.core
        self.across = (self.tp + 2) % 4

    def plane(self, x, z):
        return x * 8 + self.lo * 4 + z

    def group(self):
        return [(self.ctx, self.across), (self.partner, self.tp), (self.partner, self.across)]


def barrier_signals(me):
    sem = pltpu.get_barrier_semaphore()

    def one(k, c):
        pl.semaphore_signal(sem, inc=1, device_id=((me.ctx + k) % NB, me.tp), device_id_type=MESH)
        return c

    lax.fori_loop(1, NB, one, 0)
    for dev in ((me.ctx, me.sibling), (me.ctx, me.across), (me.partner, me.across)):
        pl.semaphore_signal(sem, inc=1, device_id=dev, device_id_type=MESH)
    return sem


def remote(src, dst, ssem, rsem, dev):
    return pltpu.make_async_remote_copy(
        src_ref=src, dst_ref=dst, send_sem=ssem, recv_sem=rsem, device_id=dev, device_id_type=MESH)


class Relay:
    def __init__(self, me, w, wg, ssem, rsem):
        self.me, self.w, self.wg, self.ssem, self.rsem = me, w, wg, ssem, rsem
        self.sends = []
        self.first = [None, None]
        self.fwd = [[None, None], [None, None]]
        self.second = [{}, {}]
        self.last = [{}, {}]

    def slot(self, h, f, s):
        me = self.me
        if h == 0:
            return ((me.x + s) % 4) * 4 + (me.z + f) % 4
        return ((me.x + f) % 4) * 4 + (me.z + s) % 4

    def dev(self, h, f, s):
        me = self.me
        if h == 0:
            return me.plane((me.x + s) % 4, (me.z + f) % 4)
        return me.plane((me.x + f) % 4, (me.z + s) % 4)

    def send(self, src, dst, dev):
        n = len(self.sends)
        c = remote(src, dst, self.ssem.at[n], self.rsem.at[n], (dev, self.me.tp))
        c.start()
        self.sends.append(c)
        return c

    def part(self, b, r, n):
        return self.wg.at[b, pl.ds(r, n), :]

    def own(self, h):
        return self.w.at[pl.ds(512 * h, 512), :]

    def pair(self, h, f):
        b = self.slot(h, f, 0)
        dst = self.part(b, 512 * h, 512)
        src = self.own(h) if f == 0 else dst
        self.second[h][f] = [self.send(src, dst, self.dev(h, 0, 1)), self.send(src, dst, self.dev(h, 0, -1))]

    def begin(self):
        for h in (0, 1):
            dst = self.part(self.slot(h, 0, 0), 512 * h, 512)
            self.first[h] = [self.send(self.own(h), dst, self.dev(h, 1, 0)), self.send(self.own(h), dst, self.dev(h, -1, 0))]

    def neighbours(self):
        for i, f in ((0, -1), (1, 1)):
            for h in (0, 1):
                self.first[h][i].wait_recv()
                part = self.part(self.slot(h, f, 0), 512 * h + 256 * i, 256)
                self.fwd[h][i] = self.send(part, part, self.dev(h, -f, 0))
                self.pair(h, f)

    def opposite(self):
        for h in (0, 1):
            for i in (0, 1):
                self.fwd[h][i].wait_recv()
            self.pair(h, 2)

    def forward(self, h, f):
        cs = []
        for i, s in ((0, -1), (1, 1)):
            self.second[h][f][i].wait_recv()
            part = self.part(self.slot(h, f, s), 512 * h + 256 * i, 256)
            cs.append(self.send(part, part, self.dev(h, 0, -s)))
        self.last[h][f] = cs

    def finish(self, h, f):
        for c in self.last[h][f]:
            c.wait_recv()


class Exchange:
    def __init__(self, me, src, dst, whole, sems):
        self.me, self.src, self.dst, self.whole, self.sems = me, src, dst, whole, sems

    def start(self):
        def go(k, c):
            to = (self.me.ctx + k) % NB
            remote(self.src(to), self.dst, self.sems[0], self.sems[1], (to, self.me.tp)).start()
            return c

        lax.fori_loop(1, NB, go, 0)

    def all(self):
        return remote(self.whole, self.whole, self.sems[0], self.sems[1], (self.me.partner, self.me.tp))


def lanes(shape):
    return lax.broadcasted_iota(jnp.int32, shape, len(shape) - 1)


def shift_matrix(SH, backward):
    for j in range(1, TAPS):
        rows = lax.broadcasted_iota(jnp.int32, (2 * T, T), 0)
        col = lanes((2 * T, T))
        source = col + j if backward else (col + (2 * T - j)) % (2 * T)
        SH[:, T * (j - 1):T * j] = jnp.where(rows == source, 1.0, 0.0).astype(BF)


def own_taps(me, cw, skip, taps, spread):
    at_block = pl.ds(at((me.ctx // 4) * T, T), T)
    rows = [cw[j, s:s + 1, at_block] for j in range(TAPS) for s in range(3)] + [skip[:, at_block]]
    rows = jnp.concatenate(rows + [jnp.zeros((T - len(rows), T), F32)], axis=0)
    taps[...] = rows.T
    own = taps[pl.ds(at((me.ctx % 4) * OWN, OWN), OWN), :]
    for n in range(3 * TAPS + 1):
        spread[n] = jnp.broadcast_to(own[:, n:n + 1], (OWN, T))


def short_conv(s, x, beside, SH, spread, blocks):
    both = jnp.concatenate([x, beside], axis=1)
    total = x.reshape(blocks, OWN, T).astype(F32) * spread[s][None]
    for p in range(3):
        moved = dot(both, SH[:, 2 * T * p:2 * T * p + 2 * T], 1, 0)
        for i in (0, 1):
            j = 2 * p + i + 1
            total = total + moved[:, T * i:T * i + T].reshape(blocks, OWN, T) * spread[3 * j + s][None]
    return total


def kernel(proj, cw_in, filt_in, skip_in, w, cot, block_out, proj_grad, filter_grad,
           cw, filt, skip, taps, spread, SF, SB, pr, wg, cotg, short, mix, longm, gated_s, gated_r, gated_t, acc,
           dgated_s, dgated_r, dmix, dshort, grad, share_s, sib_r, pre_s, share_r, hpad, M, X, D, XR, carry, gacc,
           local_s, relay_ss, relay_rs, x_ss, x_rs, cot_ss, cot_rs, pass_ss, pass_rs, sib_ss, sib_rs, share_ss, share_rs):
    me = Place()
    sem = barrier_signals(me)
    BLK = 8
    mine = pl.ds(at(OWN * me.ctx, OWN), OWN)
    half = pl.ds(at(512 * me.tp, 512), 512)

    def class_rows(lo):
        return cot.at[pl.ds(at(512 * lo, 512), 512), :]

    loads = [(cw_in, cw), (filt_in, filt), (skip_in, skip), (w, wg.at[me.x * 4 + me.z]),
             (class_rows(me.lo), cotg.at[me.lo, half, :]), (proj.at[:, mine, :], pr.at[me.ctx + 1])]
    loads = [pltpu.make_async_copy(a, b, local_s.at[n]) for n, (a, b) in enumerate(loads)]
    for c in loads:
        c.start()
    shift_matrix(SF, False)
    shift_matrix(SB, True)
    pr[0] = jnp.zeros((3, OWN, T), BF)
    for s in range(3):
        dshort[s, NB] = jnp.zeros((OWN, T), BF)
    X[:, 0:256, :] = jnp.zeros((G, 256, 256), BF)
    D[:, 256:512, :] = jnp.zeros((G, 256, 256), BF)
    pl.semaphore_wait(sem, NB - 1 + 3)

    relay = Relay(me, w, wg, relay_ss, relay_rs)
    relay.begin()
    cots = []
    for n, (ctx, tp) in enumerate(me.group()):
        lo = me.lo if n == 0 else 1 - me.lo
        cots.append(remote(class_rows(lo), cotg.at[me.lo, half, :], cot_ss.at[n], cot_rs.at[n], (ctx, tp)))
        cots[n].start()
    passes = [remote(class_rows(me.lo), cotg.at[me.lo, half, :], pass_ss.at[3], pass_rs.at[3], (me.ctx, me.sibling))]
    passes[0].start()
    for h in (0, 1):
        relay.pair(h, 0)
    proj_x = Exchange(me, lambda to: proj.at[:, pl.ds(at(OWN * to, OWN), OWN), :], pr.at[me.ctx + 1],
                      pr.at[pl.ds(1, NB - 1)], (x_ss.at[0], x_rs.at[0]))
    proj_x.start()

    for c in loads[:3]:
        c.wait()
    own_taps(me, cw, skip, taps, spread)
    build_toeplitz(filt, hpad, M)

    def skip_rows(g):
        s = spread[3 * TAPS][16 * g:16 * g + 16, :]
        s = jnp.concatenate([s, s], axis=1)
        return jnp.broadcast_to(s[None], (16, 16, 256)).reshape(256, 256)

    relay.neighbours()
    across = pl.ds(at(512 * me.across, 512), 512)
    came = [(me.lo, across), (1 - me.lo, half), (1 - me.lo, across)]
    for n, (lo, rows) in enumerate(came):
        cots[n].wait_recv()
        part = cotg.at[lo, rows, :]
        c = remote(part, part, pass_ss.at[n], pass_rs.at[n], (me.ctx, me.sibling))
        c.start()
        passes.append(c)
    for h in (0, 1):
        relay.forward(h, 0)
    relay.opposite()

    for c in loads[3:]:
        c.wait()
    proj_x.all().wait_recv()

    def short_step(r, c):
        outs = []
        for s in range(3):
            x = pr[pl.ds(BLK * r + 1, BLK), s].reshape(BLK * OWN, T)
            before = pr[pl.ds(BLK * r, BLK), s].reshape(BLK * OWN, T)
            out = short_conv(s, x, before, SF, spread, BLK).astype(BF)
            short[s, pl.ds(BLK * r, BLK)] = out
            outs.append(out.astype(F32))
        mix[pl.ds(BLK * r, BLK)] = (outs[1] * outs[2]).astype(BF)
        return c

    lax.fori_loop(0, NB // BLK, short_step, 0)
    for f in (-1, 1):
        for h in (0, 1):
            relay.forward(h, f)

    load_pairs(mix, X, 256)
    conv_forward(X, M, skip_rows, longm)
    for x in range(4):
        for b in (0, 1):
            for z in range(4):
                n = 8 * x + 4 * b + z
                gated_s[4 * x + z, b] = (short[0, n].astype(F32) * longm[n].astype(F32)).astype(BF)
    for h in (0, 1):
        relay.forward(h, 2)
    gated_x = Exchange(me, lambda to: gated_s.at[(to // 8) * 4 + to % 4], gated_r.at[me.ctx],
                       gated_r.at[pl.ds(0, NB - 1)], (x_ss.at[1], x_rs.at[1]))
    gated_x.start()
    gated_r[me.ctx] = gated_s[me.x * 4 + me.z]
    for c in passes:
        c.wait_recv()

    def slots(h, f):
        if h == 0:
            return [k * 4 + (me.z + f) % 4 for k in range(4)]
        return [((me.x + f) % 4) * 4 + k for k in range(4)]

    def product(h, f, r, right):
        left = jnp.concatenate([wg[s, r:r + 256, :] for s in slots(h, f)], axis=1)
        return dot(left, right, 1, 0)

    def columns(h, f):
        return jnp.concatenate([
            jnp.concatenate([cotg[b, pl.ds(at(s * T, T), T), :] for s in slots(h, f)], axis=0) for b in (0, 1)], axis=1)

    for f in (0, -1, 1, 2):
        for h in (0, 1):
            relay.finish(h, f)
            right = columns(h, f)
            for r in (512 * h, 512 * h + 256):
                value = product(h, f, r, right)
                if f != 0:
                    value = value + acc[r:r + 256, :]
                if f != 2:
                    acc[r:r + 256, :] = value
                    continue
                for b in (0, 1):
                    dgated_s[r // OWN:r // OWN + 8, b] = value[:, T * b:T * b + T].astype(BF).reshape(8, OWN, T)
    dgated_x = Exchange(me, lambda to: dgated_s.at[to], dgated_r.at[me.ctx], dgated_r.at[pl.ds(0, NB - 1)],
                        (x_ss.at[2], x_rs.at[2]))
    dgated_x.start()
    dgated_r[me.ctx] = dgated_s[me.ctx]

    gated_x.all().wait_recv()
    for b in (0, 1):
        for k in range(C // T):
            block = gated_r[4 * k:4 * k + 4, b].reshape(T, T).astype(F32)
            gated_t[T * b:T * b + T, T * k:T * k + T] = block.T.astype(BF)
    for x in range(4):
        for p in (0, 1):
            right = jnp.concatenate([wg[4 * x + 2 * p], wg[4 * x + 2 * p + 1]], axis=1)
            value = dot(gated_t[...], right, 1, 0).astype(BF)
            for b in (0, 1):
                share_s[x % 2, b, x // 2, :, 256 * p:256 * p + 256] = value[T * b:T * b + T, :]
    sib = remote(share_s.at[1 - me.core], sib_r, sib_ss, sib_rs, (me.ctx, me.sibling))
    sib.start()
    sib.wait_recv()
    for b in (0, 1):
        for hi in (0, 1):
            value = share_s[me.core, b, hi].astype(F32) + sib_r[b, hi].astype(F32)
            pre_s[b, hi] = value.astype(BF)
    shares = []
    for n, (ctx, tp) in enumerate(me.group()):
        b = me.lo if n == 0 else 1 - me.lo
        hi = me.hi if n == 1 else 1 - me.hi
        shares.append(remote(pre_s.at[b, hi], share_r.at[me.lo, me.hi], share_ss.at[n], share_rs.at[n], (ctx, tp)))
        shares[n].start()
    share_r[me.lo, me.hi] = pre_s[me.lo, me.hi]

    dgated_x.all().wait_recv()
    for n in range(NB):
        b, pair = (n // 4) % 2, n - n % 8 + n % 4
        value = (dgated_r[pair, b].astype(F32) + dgated_r[pair + 4, b].astype(F32)).astype(BF).astype(F32)
        dlong = (value * short[0, n].astype(F32)).astype(BF)
        for g in range(G):
            row = 16 * (n // 2)
            D[g, row:row + 16, T * (n % 2):T * (n % 2) + T] = dlong[16 * g:16 * g + 16, :]
        dshort[0, n] = (value * longm[n].astype(F32)).astype(BF)

    def grad_of(s):
        def step(r, c):
            x = dshort[s, pl.ds(BLK * r, BLK)].reshape(BLK * OWN, T)
            after = dshort[s, pl.ds(BLK * r + 1, BLK)].reshape(BLK * OWN, T)
            grad[s, pl.ds(BLK * r, BLK)] = short_conv(s, x, after, SB, spread, BLK).astype(BF)
            return c

        lax.fori_loop(0, NB // BLK, step, 0)
        moved = Exchange(me, lambda to: grad.at[s, to], proj_grad.at[s, mine, :],
                         proj_grad.at[s, pl.ds(0, C - OWN), :], (x_ss.at[3 + s], x_rs.at[3 + s]))
        moved.start()
        own = pltpu.make_async_copy(grad.at[s, me.ctx], proj_grad.at[s, mine, :], local_s.at[6 + s])
        own.start()
        return moved, own

    grads = [grad_of(0)]
    conv_backward(D, M, skip_rows, dmix)

    def dkv_step(r, c):
        at_r = pl.ds(BLK * r, BLK)
        value = dmix[at_r].astype(F32)
        for s in (1, 2):
            dshort[s, at_r] = (value * short[3 - s, at_r].astype(F32)).astype(BF)
        return c

    lax.fori_loop(0, NB // BLK, dkv_step, 0)
    grads.append(grad_of(1))
    grads.append(grad_of(2))

    filter_gradient(X, D, XR, carry, gacc, filter_grad, SCALE)
    for c in shares:
        c.wait_recv()
    for b in (0, 1):
        for k in range(4):
            cols = slice(T * k, T * k + T)
            value = share_r[b, 0, :, cols].astype(F32) + share_r[b, 1, :, cols].astype(F32)
            block_out[512 * b + T * k:512 * b + T * k + T, :] = value.T.astype(BF)
    for c in relay.sends + cots + passes + [sib] + shares:
        c.wait_send()
    for x in (proj_x, gated_x, dgated_x):
        x.all().wait_send()
    for moved, own in grads:
        own.wait()
        moved.all().wait_send()
        moved.all().wait_recv()


def local(projected, conv_weight, filters, skip_gain, out_weight, cotangent):
    dma = pltpu.SemaphoreType.DMA
    vmem = pltpu.VMEM
    blocks = vmem((NB, OWN, T), BF)
    pairs = vmem((NB, 2, OWN, T), BF)
    shares = vmem((2, 2, T, 512), BF)
    scratch = dict(
        cw=vmem((TAPS, 3, C), F32), filt=vmem((G, 4096), F32), skip=vmem((1, C), F32), taps=vmem((T, T), F32),
        spread=vmem((3 * TAPS + 1, OWN, T), F32), SF=vmem((2 * T, 6 * T), BF), SB=vmem((2 * T, 6 * T), BF),
        pr=vmem((NB + 1, 3, OWN, T), BF), wg=vmem((16, C, T), BF), cotg=vmem((2, 2048, T), BF),
        short=vmem((3, NB, OWN, T), BF), mix=blocks, longm=blocks, gated_s=vmem((16, 2, OWN, T), BF), gated_r=pairs,
        gated_t=vmem((2 * T, C), BF), acc=vmem((C, 2 * T), F32), dgated_s=pairs, dgated_r=pairs, dmix=blocks,
        dshort=vmem((3, NB + 1, OWN, T), BF), grad=vmem((3, NB, OWN, T), BF), share_s=vmem((2, 2, 2, T, 512), BF),
        sib_r=shares, pre_s=shares, share_r=shares, hpad=vmem((G, 4096 + T), F32), M=vmem((G, 256, 4096 + T), BF),
        X=vmem((G, 512, 256), BF), D=vmem((G, 512, 256), BF), XR=vmem((G, 256, 256), BF), carry=vmem((G, T, T), F32),
        gacc=vmem((G, 4352), F32), local_s=dma((9,)),
        relay_ss=dma((40,)), relay_rs=dma((40,)), x_ss=dma((6,)), x_rs=dma((6,)), cot_ss=dma((3,)), cot_rs=dma((3,)),
        pass_ss=dma((4,)), pass_rs=dma((4,)), sib_ss=dma, sib_rs=dma, share_ss=dma((3,)), share_rs=dma((3,)))
    anywhere = pl.BlockSpec(memory_space=pl.ANY)
    whole = pl.BlockSpec(memory_space=pltpu.VMEM)
    block_out, proj_grad, filter_grad = pl.pallas_call(
        kernel,
        out_shape=(
            jax.ShapeDtypeStruct((C, T), BF),
            jax.ShapeDtypeStruct((3, C, T), BF),
            jax.ShapeDtypeStruct((G, 4096), F32),
        ),
        in_specs=[anywhere] * 6,
        out_specs=(whole, anywhere, whole),
        scratch_shapes=list(scratch.values()),
        compiler_params=pltpu.CompilerParams(collective_id=1, has_side_effects=True, vmem_limit_bytes=60 << 20),
        name="hyena_block",
    )(projected, conv_weight, filters[0], skip_gain[None], out_weight, cotangent)
    return block_out, proj_grad, filter_grad[None]


def solution(mesh):
    return jax.shard_map(
        local,
        mesh=mesh,
        in_specs=(
            P(None, "tp", "ctx"),
            P(None, None, "tp"),
            P("tp", "ctx", None),
            P("tp"),
            P("tp", "ctx"),
            P("tp", "ctx"),
        ),
        out_specs=(P("tp", "ctx"), P(None, "tp", "ctx"), P("tp", "ctx", None)),
        check_vma=False,
    )
```

time: 92.7 us -> 78.3 us (0.84); the launches traced: 92.4 us -> 76.8 us
  Pallas kernels: 85.5 us -> 70.2 us
    pallas_call x1, Pallas kernels: 85.5 us -> 70.2 us  [local(): pl.pallas_call(kernel, out_shape=(jax.ShapeDtypeStruct((C, T), BF), jax.S...]
    unnamed x14 -> x6, local copies, waits for them, and re-layouts: 6.2 us -> 5.96 us
where the time goes in v4:
time: 78.3 us; the launch traced here: 76.8 us
  Pallas kernels  70.2 us (90%)
  local copies, waits for them, and re-layouts  5.96 us (8%)
    pallas_call x1, Pallas kernels, local(): pl.pallas_call(kernel, out_shape=(jax.ShapeDtypeStruct((C, T), BF), jax.S...  70.2 us
    unnamed x6, local copies, waits for them, and re-layouts  5.96 us

profile of v4, /device:TPU:0, one launch (start us, length us, event | category | flops | bytes accessed | tf_op | source)
XLA Modules:
  0.0 76.8 jit_solution(9251033546278704947)
XLA Ops:
  0.6 1.6 %copy.9.cw_in = f32[7,3,1024]{2,1,0:T(4,128)} copy(f32[7,3,1024]{2,0,1:T(8,128)} %param.7) | data formatting | bytes 172032 | tf_op args[1]
  2.2 70.2 %hyena_block.1 = (bf16[1024,128]{1,0:T(8,128)(2,1)}, bf16[3,1024,128]{2,1,0:T(8,128)(2,1)}, f32[2,4096]{1,0:T(2,128)}) custom-call(bf16[3,1024,128]{2,1,0:T(8,128)(2,1)} %proj.1, f32[7,3,1024]{2,1,0:T(4,128)} %copy.9.cw_in, f32[2,4096]{1,0:T(2,128)} %bitcast.3, f32[1,1024]{1,0:T(1,128)} %bitcast.5, bf16[1024,128]{1,0:T(8,128)(2,1)} %w.1, bf16[1024,128]{1,0:T(8,128)(2,1)} %cot.1), custom_call_target="tpu_custom_call" | custom-call | tf_op jit(solution)/shard_map/hyena_block/pallas_call | solution.py:496
  72.5 1.7 %copy.13 = bf16[1024,128]{1,0:T(8,128)(2,1)} copy(bf16[1024,128]{1,0:T(8,128)(2,1)} %get-tuple-element.12) | data formatting | bytes 524288
  74.1 0.0 copy-start
  74.1 2.1 %copy.14 = bf16[3,1024,128]{2,1,0:T(8,128)(2,1)} copy(bf16[3,1024,128]{2,1,0:T(8,128)(2,1)} %get-tuple-element.13) | data formatting | bytes 1572864
  76.2 0.0 copy-done
  76.2 0.6 copy.15
Async XLA Ops:
  74.1 2.1 %copy-start = (f32[2,4096]{1,0:T(2,128)S(1)}, f32[2,4096]{1,0:T(2,128)}, u32[]{:S(2)}) copy-start(f32[2,4096]{1,0:T(2,128)} %get-tuple-element.8) | copy-start | bytes 98308

commit v5 on v4

--- a/solution.py
+++ b/solution.py
@@ -239,7 +239,7 @@
 
 def own_taps(me, cw, skip, taps, spread):
     at_block = pl.ds(at((me.ctx // 4) * T, T), T)
-    rows = [cw[j, s:s + 1, at_block] for j in range(TAPS) for s in range(3)] + [skip[:, at_block]]
+    rows = [cw[s, j:j + 1, at_block] for j in range(TAPS) for s in range(3)] + [skip[:, at_block]]
     rows = jnp.concatenate(rows + [jnp.zeros((T - len(rows), T), F32)], axis=0)
     taps[...] = rows.T
     own = taps[pl.ds(at((me.ctx % 4) * OWN, OWN), OWN), :]
@@ -296,69 +296,11 @@
     passes[0].start()
     for h in (0, 1):
         relay.pair(h, 0)
-    proj_x = Exchange(me, lambda to: proj.at[:, pl.ds(at(OWN * to, OWN), OWN), :], pr.at[me.ctx + 1],
-                      pr.at[pl.ds(1, NB - 1)], (x_ss.at[0], x_rs.at[0]))
-    proj_x.start()
-
-    for c in loads[:3]:
-        c.wait()
-    own_taps(me, cw, skip, taps, spread)
-    build_toeplitz(filt, hpad, M)
-
     def skip_rows(g):
         s = spread[3 * TAPS][16 * g:16 * g + 16, :]
         s = jnp.concatenate([s, s], axis=1)
         return jnp.broadcast_to(s[None], (16, 16, 256)).reshape(256, 256)
 
-    relay.neighbours()
-    across = pl.ds(at(512 * me.across, 512), 512)
-    came = [(me.lo, across), (1 - me.lo, half), (1 - me.lo, across)]
-    for n, (lo, rows) in enumerate(came):
-        cots[n].wait_recv()
-        part = cotg.at[lo, rows, :]
-        c = remote(part, part, pass_ss.at[n], pass_rs.at[n], (me.ctx, me.sibling))
-        c.start()
-        passes.append(c)
-    for h in (0, 1):
-        relay.forward(h, 0)
-    relay.opposite()
-
-    for c in loads[3:]:
-        c.wait()
-    proj_x.all().wait_recv()
-
-    def short_step(r, c):
-        outs = []
-        for s in range(3):
-            x = pr[pl.ds(BLK * r + 1, BLK), s].reshape(BLK * OWN, T)
-            before = pr[pl.ds(BLK * r, BLK), s].reshape(BLK * OWN, T)
-            out = short_conv(s, x, before, SF, spread, BLK).astype(BF)
-            short[s, pl.ds(BLK * r, BLK)] = out
-            outs.append(out.astype(F32))
-        mix[pl.ds(BLK * r, BLK)] = (outs[1] * outs[2]).astype(BF)
-        return c
-
-    lax.fori_loop(0, NB // BLK, short_step, 0)
-    for f in (-1, 1):
-        for h in (0, 1):
-            relay.forward(h, f)
-
-    load_pairs(mix, X, 256)
-    conv_forward(X, M, skip_rows, longm)
-    for x in range(4):
-        for b in (0, 1):
-            for z in range(4):
-                n = 8 * x + 4 * b + z
-                gated_s[4 * x + z, b] = (short[0, n].astype(F32) * longm[n].astype(F32)).astype(BF)
-    for h in (0, 1):
-        relay.forward(h, 2)
-    gated_x = Exchange(me, lambda to: gated_s.at[(to // 8) * 4 + to % 4], gated_r.at[me.ctx],
-                       gated_r.at[pl.ds(0, NB - 1)], (x_ss.at[1], x_rs.at[1]))
-    gated_x.start()
-    gated_r[me.ctx] = gated_s[me.x * 4 + me.z]
-    for c in passes:
-        c.wait_recv()
-
     def slots(h, f):
         if h == 0:
             return [k * 4 + (me.z + f) % 4 for k in range(4)]
@@ -372,7 +314,7 @@
         return jnp.concatenate([
             jnp.concatenate([cotg[b, pl.ds(at(s * T, T), T), :] for s in slots(h, f)], axis=0) for b in (0, 1)], axis=1)
 
-    for f in (0, -1, 1, 2):
+    def contract(f):
         for h in (0, 1):
             relay.finish(h, f)
             right = columns(h, f)
@@ -385,6 +327,65 @@
                     continue
                 for b in (0, 1):
                     dgated_s[r // OWN:r // OWN + 8, b] = value[:, T * b:T * b + T].astype(BF).reshape(8, OWN, T)
+
+    proj_x = Exchange(me, lambda to: proj.at[:, pl.ds(at(OWN * to, OWN), OWN), :], pr.at[me.ctx + 1],
+                      pr.at[pl.ds(1, NB - 1)], (x_ss.at[0], x_rs.at[0]))
+    proj_x.start()
+    for c in loads[:3]:
+        c.wait()
+    own_taps(me, cw, skip, taps, spread)
+    relay.neighbours()
+    build_toeplitz(filt, hpad, M)
+    for h in (0, 1):
+        relay.forward(h, 0)
+    relay.opposite()
+    for c in loads[3:]:
+        c.wait()
+    proj_x.all().wait_recv()
+
+    def short_step(r, c):
+        outs = []
+        for s in range(3):
+            x = pr[pl.ds(BLK * r + 1, BLK), s].reshape(BLK * OWN, T)
+            before = pr[pl.ds(BLK * r, BLK), s].reshape(BLK * OWN, T)
+            out = short_conv(s, x, before, SF, spread, BLK).astype(BF)
+            short[s, pl.ds(BLK * r, BLK)] = out
+            outs.append(out.astype(F32))
+        mix[pl.ds(BLK * r, BLK)] = (outs[1] * outs[2]).astype(BF)
+        return c
+
+    lax.fori_loop(0, NB // BLK, short_step, 0)
+    across = pl.ds(at(512 * me.across, 512), 512)
+    came = [(me.lo, across), (1 - me.lo, half), (1 - me.lo, across)]
+    for n, (lo, rows) in enumerate(came):
+        cots[n].wait_recv()
+        part = cotg.at[lo, rows, :]
+        c = remote(part, part, pass_ss.at[n], pass_rs.at[n], (me.ctx, me.sibling))
+        c.start()
+        passes.append(c)
+    for h in (0, 1):
+        relay.forward(h, -1)
+    load_pairs(mix, X, 256)
+    conv_forward(X, M, skip_rows, longm)
+    for x in range(4):
+        for b in (0, 1):
+            for z in range(4):
+                n = 8 * x + 4 * b + z
+                gated_s[4 * x + z, b] = (short[0, n].astype(F32) * longm[n].astype(F32)).astype(BF)
+    for h in (0, 1):
+        relay.forward(h, 1)
+    gated_x = Exchange(me, lambda to: gated_s.at[(to // 8) * 4 + to % 4], gated_r.at[me.ctx],
+                       gated_r.at[pl.ds(0, NB - 1)], (x_ss.at[1], x_rs.at[1]))
+    gated_x.start()
+    gated_r[me.ctx] = gated_s[me.x * 4 + me.z]
+    for c in passes:
+        c.wait_recv()
+    contract(0)
+    for h in (0, 1):
+        relay.forward(h, 2)
+    contract(-1)
+    contract(1)
+    contract(2)
     dgated_x = Exchange(me, lambda to: dgated_s.at[to], dgated_r.at[me.ctx], dgated_r.at[pl.ds(0, NB - 1)],
                         (x_ss.at[2], x_rs.at[2]))
     dgated_x.start()
@@ -473,6 +474,20 @@
         moved.all().wait_recv()
 
 
+def write_results(block_in, grad_in, filter_in, block_out, proj_grad, filter_grad, block, grad, filters, sems):
+    pieces = [(grad_in.at[n], grad.at[n], proj_grad.at[n]) for n in range(3)]
+    pieces += [(block_in, block, block_out), (filter_in, filters, filter_grad)]
+    reads = [pltpu.make_async_copy(a, b, sems.at[0, n]) for n, (a, b, c) in enumerate(pieces)]
+    writes = [pltpu.make_async_copy(b, c, sems.at[1, n]) for n, (a, b, c) in enumerate(pieces)]
+    for c in reads:
+        c.start()
+    for r, c in zip(reads, writes):
+        r.wait()
+        c.start()
+    for c in writes:
+        c.wait()
+
+
 def local(projected, conv_weight, filters, skip_gain, out_weight, cotangent):
     dma = pltpu.SemaphoreType.DMA
     vmem = pltpu.VMEM
@@ -480,7 +495,7 @@
     pairs = vmem((NB, 2, OWN, T), BF)
     shares = vmem((2, 2, T, 512), BF)
     scratch = dict(
-        cw=vmem((TAPS, 3, C), F32), filt=vmem((G, 4096), F32), skip=vmem((1, C), F32), taps=vmem((T, T), F32),
+        cw=vmem((3, TAPS, C), F32), filt=vmem((G, 4096), F32), skip=vmem((1, C), F32), taps=vmem((T, T), F32),
         spread=vmem((3 * TAPS + 1, OWN, T), F32), SF=vmem((2 * T, 6 * T), BF), SB=vmem((2 * T, 6 * T), BF),
         pr=vmem((NB + 1, 3, OWN, T), BF), wg=vmem((16, C, T), BF), cotg=vmem((2, 2048, T), BF),
         short=vmem((3, NB, OWN, T), BF), mix=blocks, longm=blocks, gated_s=vmem((16, 2, OWN, T), BF), gated_r=pairs,
@@ -505,7 +520,15 @@
         scratch_shapes=list(scratch.values()),
         compiler_params=pltpu.CompilerParams(collective_id=1, has_side_effects=True, vmem_limit_bytes=60 << 20),
         name="hyena_block",
-    )(projected, conv_weight, filters[0], skip_gain[None], out_weight, cotangent)
+    )(projected, conv_weight.transpose(1, 0, 2), filters[0], skip_gain[None], out_weight, cotangent)
+    block_out, proj_grad, filter_grad = pl.pallas_call(
+        write_results,
+        out_shape=[jax.ShapeDtypeStruct(v.shape, v.dtype) for v in (block_out, proj_grad, filter_grad)],
+        in_specs=[anywhere] * 3,
+        out_specs=[anywhere] * 3,
+        scratch_shapes=[vmem((C, T), BF), vmem((3, C, T), BF), vmem((G, 4096), F32), dma((2, 5))],
+        name="write_results",
+    )(block_out, proj_grad, filter_grad)
     return block_out, proj_grad, filter_grad[None]
 
 

time: 78.3 us -> 72 us (0.920); the launches traced: 76.8 us -> 71.8 us
  local copies, waits for them, and re-layouts: 5.96 us -> 0 us
  Pallas kernels: 70.2 us -> 71.1 us
    unnamed x6 -> x0, local copies, waits for them, and re-layouts: 5.96 us -> none
    pallas_call x0 -> x1, Pallas kernels: none -> 2 us  [local(): pl.pallas_call(write_results, out_shape=[jax.ShapeDtypeStruct(v.shape, v....]
    pallas_call x1, Pallas kernels: 70.2 us -> 69.1 us  [local(): pl.pallas_call(kernel, out_shape=(jax.ShapeDtypeStruct((C, T), BF), jax.S...]
where the time goes in v5:
time: 72 us; the launch traced here: 71.8 us
  Pallas kernels  71.1 us (99%)
    pallas_call x1, Pallas kernels, local(): pl.pallas_call(kernel, out_shape=(jax.ShapeDtypeStruct((C, T), BF), jax.S...  69.1 us
    pallas_call x1, Pallas kernels, local(): pl.pallas_call(write_results, out_shape=[jax.ShapeDtypeStruct(v.shape, v....  2 us

profile of v5, /device:TPU:0, one launch (start us, length us, event | category | flops | bytes accessed | tf_op | source)
XLA Modules:
  0.0 71.8 jit_solution(7275622687162995550)
XLA Ops:
  0.6 69.1 %hyena_block.1 = (bf16[1024,128]{1,0:T(8,128)(2,1)}, bf16[3,1024,128]{2,1,0:T(8,128)(2,1)}, f32[2,4096]{1,0:T(2,128)}) custom-call(bf16[3,1024,128]{2,1,0:T(8,128)(2,1)} %proj.1, f32[3,7,1024]{2,1,0:T(8,128)} %bitcast.4, f32[2,4096]{1,0:T(2,128)} %bitcast.5, f32[1,1024]{1,0:T(1,128)} %bitcast.6, bf16[1024,128]{1,0:T(8,128)(2,1)} %w.1, bf16[1024,128]{1,0:T(8,128)(2,1)} %cot.1), custom_call_target="tpu_custom_call" | custom-call | tf_op jit(solution)/shard_map/hyena_block/pallas_call | solution.py:511
  69.8 2.0 %write_results.1 = (bf16[1024,128]{1,0:T(8,128)(2,1)}, bf16[3,1024,128]{2,1,0:T(8,128)(2,1)}, f32[2,4096]{1,0:T(2,128)}) custom-call(bf16[1024,128]{1,0:T(8,128)(2,1)} %get-tuple-element.9.block_in, bf16[3,1024,128]{2,1,0:T(8,128)(2,1)} %get-tuple-element.10.grad_in, f32[2,4096]{1,0:T(2,128)} %get-tuple-element.11.filter_in), custom_call_target="tpu_custom_call" | custom-call | tf_op jit(solution)/shard_map/write_results/pallas_call | solution.py:524

commit v6 on v5

--- a/solution.py
+++ b/solution.py
@@ -221,6 +221,14 @@
 
         lax.fori_loop(1, NB, go, 0)
 
+    def start_half(self, h):
+        def go(k, c):
+            to = 16 * h + (self.me.ctx + k) % 16
+            remote(self.src(to), self.dst, self.sems[0], self.sems[1], (to, self.me.tp)).start()
+            return c
+
+        lax.fori_loop(1 - (self.me.ctx // 16 + h) % 2, 16, go, 0)
+
     def all(self):
         return remote(self.whole, self.whole, self.sems[0], self.sems[1], (self.me.partner, self.me.tp))
 
@@ -314,6 +322,9 @@
         return jnp.concatenate([
             jnp.concatenate([cotg[b, pl.ds(at(s * T, T), T), :] for s in slots(h, f)], axis=0) for b in (0, 1)], axis=1)
 
+    dgated_x = Exchange(me, lambda to: dgated_s.at[to], dgated_r.at[me.ctx], dgated_r.at[pl.ds(0, NB - 1)],
+                        (x_ss.at[2], x_rs.at[2]))
+
     def contract(f):
         for h in (0, 1):
             relay.finish(h, f)
@@ -327,6 +338,8 @@
                     continue
                 for b in (0, 1):
                     dgated_s[r // OWN:r // OWN + 8, b] = value[:, T * b:T * b + T].astype(BF).reshape(8, OWN, T)
+            if f == 2:
+                dgated_x.start_half(h)
 
     proj_x = Exchange(me, lambda to: proj.at[:, pl.ds(at(OWN * to, OWN), OWN), :], pr.at[me.ctx + 1],
                       pr.at[pl.ds(1, NB - 1)], (x_ss.at[0], x_rs.at[0]))
@@ -386,9 +399,6 @@
     contract(-1)
     contract(1)
     contract(2)
-    dgated_x = Exchange(me, lambda to: dgated_s.at[to], dgated_r.at[me.ctx], dgated_r.at[pl.ds(0, NB - 1)],
-                        (x_ss.at[2], x_rs.at[2]))
-    dgated_x.start()
     dgated_r[me.ctx] = dgated_s[me.ctx]
 
     gated_x.all().wait_recv()
@@ -396,18 +406,22 @@
         for k in range(C // T):
             block = gated_r[4 * k:4 * k + 4, b].reshape(T, T).astype(F32)
             gated_t[T * b:T * b + T, T * k:T * k + T] = block.T.astype(BF)
-    for x in range(4):
-        for p in (0, 1):
-            right = jnp.concatenate([wg[4 * x + 2 * p], wg[4 * x + 2 * p + 1]], axis=1)
-            value = dot(gated_t[...], right, 1, 0).astype(BF)
-            for b in (0, 1):
-                share_s[x % 2, b, x // 2, :, 256 * p:256 * p + 256] = value[T * b:T * b + T, :]
-    sib = remote(share_s.at[1 - me.core], sib_r, sib_ss, sib_rs, (me.ctx, me.sibling))
-    sib.start()
+    sib = remote(share_s.at[0], sib_r, sib_ss, sib_rs, (me.ctx, me.sibling))
+    for mine_too in (0, 1):
+        parity = me.core if mine_too else 1 - me.core
+        for hi in (0, 1):
+            x = 2 * hi + parity
+            for p in (0, 1):
+                right = jnp.concatenate([wg[4 * x + 2 * p], wg[4 * x + 2 * p + 1]], axis=1)
+                value = dot(gated_t[...], right, 1, 0).astype(BF)
+                for b in (0, 1):
+                    share_s[mine_too, b, hi, :, 256 * p:256 * p + 256] = value[T * b:T * b + T, :]
+        if not mine_too:
+            sib.start()
     sib.wait_recv()
     for b in (0, 1):
         for hi in (0, 1):
-            value = share_s[me.core, b, hi].astype(F32) + sib_r[b, hi].astype(F32)
+            value = share_s[1, b, hi].astype(F32) + sib_r[b, hi].astype(F32)
             pre_s[b, hi] = value.astype(BF)
     shares = []
     for n, (ctx, tp) in enumerate(me.group()):
@@ -427,22 +441,24 @@
             D[g, row:row + 16, T * (n % 2):T * (n % 2) + T] = dlong[16 * g:16 * g + 16, :]
         dshort[0, n] = (value * longm[n].astype(F32)).astype(BF)
 
-    def grad_of(s):
+    def grad_of(streams, n):
         def step(r, c):
-            x = dshort[s, pl.ds(BLK * r, BLK)].reshape(BLK * OWN, T)
-            after = dshort[s, pl.ds(BLK * r + 1, BLK)].reshape(BLK * OWN, T)
-            grad[s, pl.ds(BLK * r, BLK)] = short_conv(s, x, after, SB, spread, BLK).astype(BF)
+            for s in streams:
+                x = dshort[s, pl.ds(BLK * r, BLK)].reshape(BLK * OWN, T)
+                after = dshort[s, pl.ds(BLK * r + 1, BLK)].reshape(BLK * OWN, T)
+                grad[pl.ds(BLK * r, BLK), s] = short_conv(s, x, after, SB, spread, BLK).astype(BF)
             return c
 
         lax.fori_loop(0, NB // BLK, step, 0)
-        moved = Exchange(me, lambda to: grad.at[s, to], proj_grad.at[s, mine, :],
-                         proj_grad.at[s, pl.ds(0, C - OWN), :], (x_ss.at[3 + s], x_rs.at[3 + s]))
+        some = pl.ds(streams[0], len(streams))
+        moved = Exchange(me, lambda to: grad.at[to, some], proj_grad.at[some, mine, :],
+                         proj_grad.at[some, pl.ds(0, C - OWN), :], (x_ss.at[3 + n], x_rs.at[3 + n]))
         moved.start()
-        own = pltpu.make_async_copy(grad.at[s, me.ctx], proj_grad.at[s, mine, :], local_s.at[6 + s])
+        own = pltpu.make_async_copy(grad.at[me.ctx, some], proj_grad.at[some, mine, :], local_s.at[6 + n])
         own.start()
         return moved, own
 
-    grads = [grad_of(0)]
+    grads = [grad_of((0,), 0)]
     conv_backward(D, M, skip_rows, dmix)
 
     def dkv_step(r, c):
@@ -453,8 +469,7 @@
         return c
 
     lax.fori_loop(0, NB // BLK, dkv_step, 0)
-    grads.append(grad_of(1))
-    grads.append(grad_of(2))
+    grads.append(grad_of((1, 2), 1))
 
     filter_gradient(X, D, XR, carry, gacc, filter_grad, SCALE)
     for c in shares:
@@ -475,8 +490,9 @@
 
 
 def write_results(block_in, grad_in, filter_in, block_out, proj_grad, filter_grad, block, grad, filters, sems):
-    pieces = [(grad_in.at[n], grad.at[n], proj_grad.at[n]) for n in range(3)]
-    pieces += [(block_in, block, block_out), (filter_in, filters, filter_grad)]
+    cuts = [pl.ds(256 * n, 256) for n in range(4)]
+    pieces = [(grad_in.at[n, c], grad.at[n, c], proj_grad.at[n, c]) for n in range(3) for c in cuts]
+    pieces += [(block_in.at[c], block.at[c], block_out.at[c]) for c in cuts] + [(filter_in, filters, filter_grad)]
     reads = [pltpu.make_async_copy(a, b, sems.at[0, n]) for n, (a, b, c) in enumerate(pieces)]
     writes = [pltpu.make_async_copy(b, c, sems.at[1, n]) for n, (a, b, c) in enumerate(pieces)]
     for c in reads:
@@ -500,7 +516,7 @@
         pr=vmem((NB + 1, 3, OWN, T), BF), wg=vmem((16, C, T), BF), cotg=vmem((2, 2048, T), BF),
         short=vmem((3, NB, OWN, T), BF), mix=blocks, longm=blocks, gated_s=vmem((16, 2, OWN, T), BF), gated_r=pairs,
         gated_t=vmem((2 * T, C), BF), acc=vmem((C, 2 * T), F32), dgated_s=pairs, dgated_r=pairs, dmix=blocks,
-        dshort=vmem((3, NB + 1, OWN, T), BF), grad=vmem((3, NB, OWN, T), BF), share_s=vmem((2, 2, 2, T, 512), BF),
+        dshort=vmem((3, NB + 1, OWN, T), BF), grad=vmem((NB, 3, OWN, T), BF), share_s=vmem((2, 2, 2, T, 512), BF),
         sib_r=shares, pre_s=shares, share_r=shares, hpad=vmem((G, 4096 + T), F32), M=vmem((G, 256, 4096 + T), BF),
         X=vmem((G, 512, 256), BF), D=vmem((G, 512, 256), BF), XR=vmem((G, 256, 256), BF), carry=vmem((G, T, T), F32),
         gacc=vmem((G, 4352), F32), local_s=dma((9,)),
@@ -526,7 +542,7 @@
         out_shape=[jax.ShapeDtypeStruct(v.shape, v.dtype) for v in (block_out, proj_grad, filter_grad)],
         in_specs=[anywhere] * 3,
         out_specs=[anywhere] * 3,
-        scratch_shapes=[vmem((C, T), BF), vmem((3, C, T), BF), vmem((G, 4096), F32), dma((2, 5))],
+        scratch_shapes=[vmem((C, T), BF), vmem((3, C, T), BF), vmem((G, 4096), F32), dma((2, 17))],
         name="write_results",
     )(block_out, proj_grad, filter_grad)
     return block_out, proj_grad, filter_grad[None]

time: 72 us -> 71.9 us (level)
  no operation moved by 1% of the time
where the time goes in v6:
time: 71.9 us; the launch traced here: 71.7 us
  Pallas kernels  71.1 us (99%)
    pallas_call x1, Pallas kernels, local(): pl.pallas_call(kernel, out_shape=(jax.ShapeDtypeStruct((C, T), BF), jax.S...  68.9 us
    pallas_call x1, Pallas kernels, local(): pl.pallas_call(write_results, out_shape=[jax.ShapeDtypeStruct(v.shape, v....  2.18 us

profile of v6, /device:TPU:0, one launch (start us, length us, event | category | flops | bytes accessed | tf_op | source)
XLA Modules:
  0.0 71.7 jit_solution(1413596571114603979)
XLA Ops:
  0.6 68.9 %hyena_block.1 = (bf16[1024,128]{1,0:T(8,128)(2,1)}, bf16[3,1024,128]{2,1,0:T(8,128)(2,1)}, f32[2,4096]{1,0:T(2,128)}) custom-call(bf16[3,1024,128]{2,1,0:T(8,128)(2,1)} %proj.1, f32[3,7,1024]{2,1,0:T(8,128)} %bitcast.4, f32[2,4096]{1,0:T(2,128)} %bitcast.5, f32[1,1024]{1,0:T(1,128)} %bitcast.6, bf16[1024,128]{1,0:T(8,128)(2,1)} %w.1, bf16[1024,128]{1,0:T(8,128)(2,1)} %cot.1), custom_call_target="tpu_custom_call" | custom-call | tf_op jit(solution)/shard_map/hyena_block/pallas_call | solution.py:527
  69.5 2.2 %write_results.1 = (bf16[1024,128]{1,0:T(8,128)(2,1)}, bf16[3,1024,128]{2,1,0:T(8,128)(2,1)}, f32[2,4096]{1,0:T(2,128)}) custom-call(bf16[1024,128]{1,0:T(8,128)(2,1)} %get-tuple-element.9.block_in, bf16[3,1024,128]{2,1,0:T(8,128)(2,1)} %get-tuple-element.10.grad_in, f32[2,4096]{1,0:T(2,128)} %get-tuple-element.11.filter_in), custom_call_target="tpu_custom_call" | custom-call | tf_op jit(solution)/shard_map/write_results/pallas_call | solution.py:540

commit v7 on v6

--- a/solution.py
+++ b/solution.py
@@ -267,7 +267,7 @@
 
 
 def kernel(proj, cw_in, filt_in, skip_in, w, cot, block_out, proj_grad, filter_grad,
-           cw, filt, skip, taps, spread, SF, SB, pr, wg, cotg, short, mix, longm, gated_s, gated_r, gated_t, acc,
+           cw, filt, skip, taps, spread, SF, SB, pr, pv, wg, cotg, short, mix, longm, gated_s, gated_r, gated_t, acc,
            dgated_s, dgated_r, dmix, dshort, grad, share_s, sib_r, pre_s, share_r, hpad, M, X, D, XR, carry, gacc,
            local_s, relay_ss, relay_rs, x_ss, x_rs, cot_ss, cot_rs, pass_ss, pass_rs, sib_ss, sib_rs, share_ss, share_rs):
     me = Place()
@@ -280,7 +280,7 @@
         return cot.at[pl.ds(at(512 * lo, 512), 512), :]
 
     loads = [(cw_in, cw), (filt_in, filt), (skip_in, skip), (w, wg.at[me.x * 4 + me.z]),
-             (class_rows(me.lo), cotg.at[me.lo, half, :]), (proj.at[:, mine, :], pr.at[me.ctx + 1])]
+             (class_rows(me.lo), cotg.at[me.lo, half, :]), (proj.at[:, mine, :], pr.at[me.ctx + 1]), (proj, pv)]
     loads = [pltpu.make_async_copy(a, b, local_s.at[n]) for n, (a, b) in enumerate(loads)]
     for c in loads:
         c.start()
@@ -293,7 +293,9 @@
     D[:, 256:512, :] = jnp.zeros((G, 256, 256), BF)
     pl.semaphore_wait(sem, NB - 1 + 3)
 
-    relay = Relay(me, w, wg, relay_ss, relay_rs)
+    loads[3].wait()
+    loads[6].wait()
+    relay = Relay(me, wg.at[me.x * 4 + me.z], wg, relay_ss, relay_rs)
     relay.begin()
     cots = []
     for n, (ctx, tp) in enumerate(me.group()):
@@ -341,7 +343,7 @@
             if f == 2:
                 dgated_x.start_half(h)
 
-    proj_x = Exchange(me, lambda to: proj.at[:, pl.ds(at(OWN * to, OWN), OWN), :], pr.at[me.ctx + 1],
+    proj_x = Exchange(me, lambda to: pv.at[:, pl.ds(at(OWN * to, OWN), OWN), :], pr.at[me.ctx + 1],
                       pr.at[pl.ds(1, NB - 1)], (x_ss.at[0], x_rs.at[0]))
     proj_x.start()
     for c in loads[:3]:
@@ -352,7 +354,7 @@
     for h in (0, 1):
         relay.forward(h, 0)
     relay.opposite()
-    for c in loads[3:]:
+    for c in loads[4:6]:
         c.wait()
     proj_x.all().wait_recv()
 
@@ -454,7 +456,7 @@
         moved = Exchange(me, lambda to: grad.at[to, some], proj_grad.at[some, mine, :],
                          proj_grad.at[some, pl.ds(0, C - OWN), :], (x_ss.at[3 + n], x_rs.at[3 + n]))
         moved.start()
-        own = pltpu.make_async_copy(grad.at[me.ctx, some], proj_grad.at[some, mine, :], local_s.at[6 + n])
+        own = pltpu.make_async_copy(grad.at[me.ctx, some], proj_grad.at[some, mine, :], local_s.at[7 + n])
         own.start()
         return moved, own
 
@@ -490,9 +492,8 @@
 
 
 def write_results(block_in, grad_in, filter_in, block_out, proj_grad, filter_grad, block, grad, filters, sems):
-    cuts = [pl.ds(256 * n, 256) for n in range(4)]
-    pieces = [(grad_in.at[n, c], grad.at[n, c], proj_grad.at[n, c]) for n in range(3) for c in cuts]
-    pieces += [(block_in.at[c], block.at[c], block_out.at[c]) for c in cuts] + [(filter_in, filters, filter_grad)]
+    pieces = [(grad_in.at[n], grad.at[n], proj_grad.at[n]) for n in range(3)]
+    pieces += [(block_in, block, block_out), (filter_in, filters, filter_grad)]
     reads = [pltpu.make_async_copy(a, b, sems.at[0, n]) for n, (a, b, c) in enumerate(pieces)]
     writes = [pltpu.make_async_copy(b, c, sems.at[1, n]) for n, (a, b, c) in enumerate(pieces)]
     for c in reads:
@@ -513,13 +514,13 @@
     scratch = dict(
         cw=vmem((3, TAPS, C), F32), filt=vmem((G, 4096), F32), skip=vmem((1, C), F32), taps=vmem((T, T), F32),
         spread=vmem((3 * TAPS + 1, OWN, T), F32), SF=vmem((2 * T, 6 * T), BF), SB=vmem((2 * T, 6 * T), BF),
-        pr=vmem((NB + 1, 3, OWN, T), BF), wg=vmem((16, C, T), BF), cotg=vmem((2, 2048, T), BF),
+        pr=vmem((NB + 1, 3, OWN, T), BF), pv=vmem((3, C, T), BF), wg=vmem((16, C, T), BF), cotg=vmem((2, 2048, T), BF),
         short=vmem((3, NB, OWN, T), BF), mix=blocks, longm=blocks, gated_s=vmem((16, 2, OWN, T), BF), gated_r=pairs,
         gated_t=vmem((2 * T, C), BF), acc=vmem((C, 2 * T), F32), dgated_s=pairs, dgated_r=pairs, dmix=blocks,
         dshort=vmem((3, NB + 1, OWN, T), BF), grad=vmem((NB, 3, OWN, T), BF), share_s=vmem((2, 2, 2, T, 512), BF),
         sib_r=shares, pre_s=shares, share_r=shares, hpad=vmem((G, 4096 + T), F32), M=vmem((G, 256, 4096 + T), BF),
         X=vmem((G, 512, 256), BF), D=vmem((G, 512, 256), BF), XR=vmem((G, 256, 256), BF), carry=vmem((G, T, T), F32),
-        gacc=vmem((G, 4352), F32), local_s=dma((9,)),
+        gacc=vmem((G, 4352), F32), local_s=dma((10,)),
         relay_ss=dma((40,)), relay_rs=dma((40,)), x_ss=dma((6,)), x_rs=dma((6,)), cot_ss=dma((3,)), cot_rs=dma((3,)),
         pass_ss=dma((4,)), pass_rs=dma((4,)), sib_ss=dma, sib_rs=dma, share_ss=dma((3,)), share_rs=dma((3,)))
     anywhere = pl.BlockSpec(memory_space=pl.ANY)
@@ -542,7 +543,7 @@
         out_shape=[jax.ShapeDtypeStruct(v.shape, v.dtype) for v in (block_out, proj_grad, filter_grad)],
         in_specs=[anywhere] * 3,
         out_specs=[anywhere] * 3,
-        scratch_shapes=[vmem((C, T), BF), vmem((3, C, T), BF), vmem((G, 4096), F32), dma((2, 17))],
+        scratch_shapes=[vmem((C, T), BF), vmem((3, C, T), BF), vmem((G, 4096), F32), dma((2, 5))],
         name="write_results",
     )(block_out, proj_grad, filter_grad)
     return block_out, proj_grad, filter_grad[None]

time: 71.9 us -> 71.5 us (level)
  no operation moved by 1% of the time
where the time goes in v7:
time: 71.5 us; the launch traced here: 71.3 us
  Pallas kernels  70.7 us (99%)
    pallas_call x1, Pallas kernels, local(): pl.pallas_call(kernel, out_shape=(jax.ShapeDtypeStruct((C, T), BF), jax.S...  68.7 us
    pallas_call x1, Pallas kernels, local(): pl.pallas_call(write_results, out_shape=[jax.ShapeDtypeStruct(v.shape, v....  2 us

profile of v7, /device:TPU:0, one launch (start us, length us, event | category | flops | bytes accessed | tf_op | source)
XLA Modules:
  0.0 71.3 jit_solution(2077847652523547190)
XLA Ops:
  0.6 68.7 %hyena_block.1 = (bf16[1024,128]{1,0:T(8,128)(2,1)}, bf16[3,1024,128]{2,1,0:T(8,128)(2,1)}, f32[2,4096]{1,0:T(2,128)}) custom-call(bf16[3,1024,128]{2,1,0:T(8,128)(2,1)} %proj.1, f32[3,7,1024]{2,1,0:T(8,128)} %bitcast.4, f32[2,4096]{1,0:T(2,128)} %bitcast.5, f32[1,1024]{1,0:T(1,128)} %bitcast.6, bf16[1024,128]{1,0:T(8,128)(2,1)} %w.1, bf16[1024,128]{1,0:T(8,128)(2,1)} %cot.1), custom_call_target="tpu_custom_call" | custom-call | tf_op jit(solution)/shard_map/hyena_block/pallas_call | solution.py:528
  69.3 2.0 %write_results.1 = (bf16[1024,128]{1,0:T(8,128)(2,1)}, bf16[3,1024,128]{2,1,0:T(8,128)(2,1)}, f32[2,4096]{1,0:T(2,128)}) custom-call(bf16[1024,128]{1,0:T(8,128)(2,1)} %get-tuple-element.9.block_in, bf16[3,1024,128]{2,1,0:T(8,128)(2,1)} %get-tuple-element.10.grad_in, f32[2,4096]{1,0:T(2,128)} %get-tuple-element.11.filter_in), custom_call_target="tpu_custom_call" | custom-call | tf_op jit(solution)/shard_map/write_results/pallas_call | solution.py:541
